TPU v7x, 32 devices: a whole 2x2x4 slice. The times are simulated.
32 devices in a mesh: dp: 8 (over y, x, core), section: 4 (over z).
Axes of the slice: x: 2, y: 2, z: 4, core: 2. Of those that a mesh axis runs over, the one named last changes fastest.
Arguments:
- images: bfloat16 [6, 32, 196, 384], P(None, 'dp'), may hold values from -6 to 6
- out_grad: bfloat16 [6, 32, 196, 384], P(None, 'dp'), may hold values from -6 to 6
- padding: int32 [6, 32], P(None, 'dp'), may hold values 0 or 1
- affine_scale: bfloat16 [4, 384], replicated, may hold values from 0.5 to 1.5
- affine_shift: bfloat16 [4, 384], replicated, may hold values from -3 to 3
- layer_scale: bfloat16 [4, 384], replicated, may hold values from 0.29882812 to 1.5
- patch_weight: bfloat16 [2, 196, 196], replicated, may hold values from -0.4375 to 0.4375
- patch_bias: bfloat16 [2, 196], replicated, may hold values from -3 to 3
- up_weight: bfloat16 [2, 384, 1536], replicated, may hold values from -0.3125 to 0.3125
- up_bias: bfloat16 [2, 1536], replicated, may hold values from -3 to 3
- down_weight: bfloat16 [2, 1536, 384], replicated, may hold values from -0.15625 to 0.15625
- down_bias: bfloat16 [2, 384], replicated, may hold values from -2 to 2
Outputs:
- section_outputs: bfloat16 [4, 6, 32, 196, 384], P('section', None, 'dp')
- section_input_grads: bfloat16 [4, 6, 32, 196, 384], P('section', None, 'dp')
- scale_grads: float32 [4, 384], replicated
- shift_grads: float32 [4, 384], replicated
- gain_grads: float32 [4, 384], replicated
- tile_projection_slopes: float32 [2, 196, 196], replicated
- offset_grads: float32 [2, 196], replicated
- upward_grads: float32 [2, 384, 1536], replicated
- upbias_grads: float32 [2, 1536], replicated
- downward_grads: float32 [2, 1536, 384], replicated
- downbias_grads: float32 [2, 384], replicated
All inputs are finite; a program needn't handle non-finite values. No bound on the sum of `padding` on one device may be relied on, other than what follows from the above.
Results may differ from a plain program's by a relative error of at most 0.012.
The roundings to bfloat16 on the way count: a program that leaves them out, or rounds other values in their place, can miss the bound.
Values may be sent and summed in bfloat16 or wider, within the bound.
A program may use at most 128 MiB of HBM per device.

v0:
```python
import jax
import jax.numpy as jnp
from jax import lax
from jax.sharding import PartitionSpec as P


def for_sending(value):
    return jax.tree.map(lambda a: a.astype(jnp.bfloat16) if a.dtype == jnp.float32 else a, value)


def from_behind(value, axis, steps):
    count = lax.axis_size(axis)
    initial, last = (max(0, -steps), min(count, count - steps))
    return lax.ppermute(value, axis, [(source, source + steps) for source in range(initial, last)])


def pick(table, index):
    return lax.dynamic_index_in_dim(table, index, 0, keepdims=False)


def shards(
    images,
    out_grad,
    padding,
    affine_scale,
    affine_shift,
    layer_scale,
    patch_weight,
    patch_bias,
    up_weight,
    up_bias,
    down_weight,
    down_bias,
):
    section = lax.axis_index("section")
    n_section = lax.axis_size("section")
    layer = section // 2
    micro_count = images.shape[0]
    n_layer = patch_weight.shape[0]
    alpha = pick(affine_scale, section).astype(jnp.float32)
    beta = pick(affine_shift, section).astype(jnp.float32)
    gain = pick(layer_scale, section).astype(jnp.float32)
    token_blend_table = pick(patch_weight, layer)
    mixbias = pick(patch_bias, layer).astype(jnp.float32)
    w_up = pick(up_weight, layer)
    b_up = pick(up_bias, layer).astype(jnp.float32)
    w_down = pick(down_weight, layer)
    b_down = pick(down_bias, layer).astype(jnp.float32)
    live = padding.astype(jnp.float32)

    def patch_mix(xin):
        xfull = xin.astype(jnp.float32)
        normalized_input = (alpha * xfull + beta).astype(jnp.bfloat16)
        mixing_output = (
            jnp.einsum(
                "nk,gkw->gnw",
                token_blend_table,
                normalized_input,
                preferred_element_type=jnp.float32,
            )
            + mixbias[None, :, None]
        )
        return (xfull, normalized_input, mixing_output)

    def channel_mix(xin):
        xfull = xin.astype(jnp.float32)
        normalized_input = (alpha * xfull + beta).astype(jnp.bfloat16)
        pre = (
            jnp.einsum("bpd,dh->bph", normalized_input, w_up, preferred_element_type=jnp.float32)
            + b_up
        )
        value, slope = jax.vjp(jax.nn.gelu, pre)
        hidden = value.astype(jnp.bfloat16)
        residual_path = (
            jnp.einsum("bph,hd->bpd", hidden, w_down, preferred_element_type=jnp.float32) + b_down
        )
        return (xfull, normalized_input, hidden, slope, residual_path)

    def skip_forward(xin):
        return jnp.zeros_like(xin)

    def patch_forward(xin):
        xfull, normalized_input, mixing_output = patch_mix(xin)
        return (xfull + gain * mixing_output).astype(jnp.bfloat16)

    def channel_forward(xin):
        xfull, normalized_input, hidden, slope, residual_path = channel_mix(xin)
        return (xfull + gain * residual_path).astype(jnp.bfloat16)

    empty = (
        jnp.zeros_like(alpha),
        jnp.zeros_like(alpha),
        jnp.zeros_like(alpha),
        jnp.zeros(token_blend_table.shape, jnp.float32),
        jnp.zeros_like(mixbias),
        jnp.zeros(w_up.shape, jnp.float32),
        jnp.zeros_like(b_up),
        jnp.zeros(w_down.shape, jnp.float32),
        jnp.zeros_like(b_down),
    )

    def skip_backward(xin, gout):
        return (jnp.zeros_like(xin), empty)

    def patch_backward(xin, gout):
        xfull, normalized_input, mixing_output = patch_mix(xin)
        grad = gout.astype(jnp.float32)
        g_gain = jnp.sum(grad * mixing_output, axis=(0, 1))
        token_blend_product = (gain * grad).astype(jnp.bfloat16)
        token_blend_coefficient_slope = jnp.einsum(
            "xsh,xfh->sf", token_blend_product, normalized_input, preferred_element_type=jnp.float32
        )
        g_mixbias = jnp.sum(token_blend_product.astype(jnp.float32), axis=(0, 2))
        normalized_gradient = jnp.einsum(
            "cq,vcu->vqu",
            token_blend_table,
            token_blend_product,
            preferred_element_type=jnp.float32,
        )
        g_alpha = jnp.sum(normalized_gradient * xfull, axis=(0, 1))
        g_beta = jnp.sum(normalized_gradient, axis=(0, 1))
        dx = (grad + alpha * normalized_gradient).astype(jnp.bfloat16)
        return (
            dx,
            (
                g_alpha,
                g_beta,
                g_gain,
                token_blend_coefficient_slope,
                g_mixbias,
                empty[5],
                empty[6],
                empty[7],
                empty[8],
            ),
        )

    def channel_backward(xin, gout):
        xfull, normalized_input, hidden, slope, residual_path = channel_mix(xin)
        grad = gout.astype(jnp.float32)
        g_gain = jnp.sum(grad * residual_path, axis=(0, 1))
        ebranch = (gain * grad).astype(jnp.bfloat16)
        g_down = jnp.einsum("bph,bpd->hd", hidden, ebranch, preferred_element_type=jnp.float32)
        lowering_offset_slope = jnp.sum(ebranch.astype(jnp.float32), axis=(0, 1))
        dhidden = jnp.einsum("bpd,hd->bph", ebranch, w_down, preferred_element_type=jnp.float32)
        dpre = slope(dhidden)[0].astype(jnp.bfloat16)
        g_up = jnp.einsum("bpd,bph->dh", normalized_input, dpre, preferred_element_type=jnp.float32)
        g_upb = jnp.sum(dpre.astype(jnp.float32), axis=(0, 1))
        normalized_gradient = jnp.einsum(
            "bph,dh->bpd", dpre, w_up, preferred_element_type=jnp.float32
        )
        g_alpha = jnp.sum(normalized_gradient * xfull, axis=(0, 1))
        g_beta = jnp.sum(normalized_gradient, axis=(0, 1))
        dx = (grad + alpha * normalized_gradient).astype(jnp.bfloat16)
        return (
            dx,
            (
                g_alpha,
                g_beta,
                g_gain,
                empty[3],
                empty[4],
                g_up,
                g_upb,
                g_down,
                lowering_offset_slope,
            ),
        )

    def forward_tick(tick, carry):
        incoming, kept, outputs = carry
        micro = tick - section
        valid = (micro >= 0) & (micro < micro_count)
        slot = jnp.clip(micro, 0, micro_count - 1)
        fresh = (images[slot].astype(jnp.float32) * live[slot][:, None, None]).astype(jnp.bfloat16)
        xin = jnp.where(section == 0, fresh, incoming)
        which = jnp.where(valid, 1 + section % 2, 0)
        result = lax.switch(which, (skip_forward, patch_forward, channel_forward), xin)
        kept = lax.dynamic_update_index_in_dim(kept, jnp.where(valid, xin, kept[slot]), slot, 0)
        outputs = lax.dynamic_update_index_in_dim(
            outputs, jnp.where(valid, result, outputs[slot]), slot, 0
        )
        incoming = jax.tree.map(
            lambda part, own: part.astype(own.dtype),
            from_behind(for_sending(result), "section", 1),
            result,
        )
        return (incoming, kept, outputs)

    zero_block = jnp.zeros(images.shape[1:], jnp.bfloat16)
    ticks = micro_count + n_section - 1
    start = (zero_block, jnp.zeros_like(images), jnp.zeros_like(images))
    unused, kept, outputs = lax.fori_loop(0, ticks, forward_tick, start)

    def backward_tick(tick, carry):
        incoming, in_grads, totals = carry
        micro = tick - (n_section - 1 - section)
        valid = (micro >= 0) & (micro < micro_count)
        slot = jnp.clip(micro, 0, micro_count - 1)
        fresh = (out_grad[slot].astype(jnp.float32) * live[slot][:, None, None]).astype(
            jnp.bfloat16
        )
        gout = jnp.where(section == n_section - 1, fresh, incoming)
        which = jnp.where(valid, 1 + section % 2, 0)
        dx, grads = lax.switch(
            which, (skip_backward, patch_backward, channel_backward), kept[slot], gout
        )
        totals = jax.tree.map(lambda left, right: left + right, totals, grads)
        in_grads = lax.dynamic_update_index_in_dim(
            in_grads, jnp.where(valid, dx, in_grads[slot]), slot, 0
        )
        incoming = jax.tree.map(
            lambda part, own: part.astype(own.dtype),
            from_behind(for_sending(dx), "section", -1),
            dx,
        )
        return (incoming, in_grads, totals)

    unused, in_grads, totals = lax.fori_loop(
        0, ticks, backward_tick, (zero_block, jnp.zeros_like(images), empty)
    )
    (
        g_alpha,
        g_beta,
        g_gain,
        token_blend_coefficient_slope,
        g_mixbias,
        g_up,
        g_upb,
        g_down,
        lowering_offset_slope,
    ) = totals
    on_section = (jnp.arange(n_section) == section).astype(jnp.float32)[:, None]
    on_layer = (jnp.arange(n_layer) == layer).astype(jnp.float32)
    summed = lax.psum(
        (
            on_section * g_alpha,
            on_section * g_beta,
            on_section * g_gain,
            on_layer[:, None, None] * token_blend_coefficient_slope,
            on_layer[:, None] * g_mixbias,
            on_layer[:, None, None] * g_up,
            on_layer[:, None] * g_upb,
            on_layer[:, None, None] * g_down,
            on_layer[:, None] * lowering_offset_slope,
        ),
        ("dp", "section"),
    )
    scale_g, shift_g, gain_g, mixer_g, mixbias_g, up_g, upb_g, down_g, downb_g = summed
    return (
        outputs[None],
        in_grads[None],
        scale_g,
        shift_g,
        gain_g,
        mixer_g,
        mixbias_g,
        up_g,
        upb_g,
        down_g,
        downb_g,
    )


def solution(mesh):
    return jax.shard_map(
        shards,
        mesh=mesh,
        in_specs=(
            P(None, "dp", None, None),
            P(None, "dp", None, None),
            P(None, "dp"),
            P(),
            P(),
            P(),
            P(),
            P(),
            P(),
            P(),
            P(),
            P(),
        ),
        out_specs=(
            P("section", None, "dp", None, None),
            P("section", None, "dp", None, None),
            P(),
            P(),
            P(),
            P(),
            P(),
            P(),
            P(),
            P(),
            P(),
        ),
        check_vma=False,
    )
```

profile of v0, /device:TPU:0, one launch (start us, length us, event | category | flops | bytes accessed | tf_op | source)
XLA Modules:
  0.0 803.9 jit_solution(13455345268795514270)
XLA Ops:
  12.6 2.7 broadcast.94.clone2
  15.3 2.7 broadcast.94.clone2.1
  18.2 194.1 %while.55 = (s32[]{:T(128)}, bf16[4,196,384]{2,0,1:T(4,128)(2,1)S(1)}, bf16[6,4,196,384]{3,1,2,0:T(4,128)(2,1)}, bf16[6,4,196,384]{3,1,2,0:T(4,128)(2,1)}, s32[]...) while((s32[]{:T(128)}, ...), condition=%wide.region_4.5_spmd, body=%wide.region_0.4_spmd.sunk | while | flops 1866246144 | bytes 14414857 | solution.py:193
  19.6 2.6 bitcast_dynamic-update-slice_fusion.4
  22.8 4.5 collective-permute-start
  29.7 10.4 %collective-permute-done = bf16[4,196,384]{2,0,1:T(4,128)(2,1)S(1)} collective-permute-done((bf16[4,196,384]{2,0,1:T(4,128)(2,1)S(1)}, bf16[4,196,384]{2,0,1:T(4,128)(2,1)S(1)}, u32[]{:S(2)}, u32[]{:S(2)}) %collective-permute-start) | collective-permute-done | bytes 602144 | tf_op jit(solution)/shard_map/while/body/eval_jaxpr/ppermute | solution.py:14
  41.4 2.6 bitcast_dynamic-update-slice_fusion.4
  44.6 9.2 %collective-permute-start = (bf16[4,196,384]{2,0,1:T(4,128)(2,1)S(1)}, bf16[4,196,384]{2,0,1:T(4,128)(2,1)S(1)}, u32[]{:S(2)}, u32[]{:S(2)}) collective-permute-start(bf16[4,196,384]{2,0,1:T(4,128)(2,1)S(1)} %get-tuple-element.1716), channel_id=1, source_target_pairs={{0,1},{1,2},{2,3},{4,5},{5,6},{6,7},{8,9},{9,10},{10,11},{12,13},{... | collective-permute-start | bytes 1806344 | tf_op jit(solution)/shard_map/while/body/eval_jaxpr/ppermute | solution.py:14
  56.2 9.5 %collective-permute-done = bf16[4,196,384]{2,0,1:T(4,128)(2,1)S(1)} collective-permute-done((bf16[4,196,384]{2,0,1:T(4,128)(2,1)S(1)}, bf16[4,196,384]{2,0,1:T(4,128)(2,1)S(1)}, u32[]{:S(2)}, u32[]{:S(2)}) %collective-permute-start) | collective-permute-done | bytes 602144 | tf_op jit(solution)/shard_map/while/body/eval_jaxpr/ppermute | solution.py:14
  67.0 2.6 bitcast_dynamic-update-slice_fusion.4
  70.3 9.2 %collective-permute-start = (bf16[4,196,384]{2,0,1:T(4,128)(2,1)S(1)}, bf16[4,196,384]{2,0,1:T(4,128)(2,1)S(1)}, u32[]{:S(2)}, u32[]{:S(2)}) collective-permute-start(bf16[4,196,384]{2,0,1:T(4,128)(2,1)S(1)} %get-tuple-element.1716), channel_id=1, source_target_pairs={{0,1},{1,2},{2,3},{4,5},{5,6},{6,7},{8,9},{9,10},{10,11},{12,13},{... | collective-permute-start | bytes 1806344 | tf_op jit(solution)/shard_map/while/body/eval_jaxpr/ppermute | solution.py:14
  81.9 8.6 %collective-permute-done = bf16[4,196,384]{2,0,1:T(4,128)(2,1)S(1)} collective-permute-done((bf16[4,196,384]{2,0,1:T(4,128)(2,1)S(1)}, bf16[4,196,384]{2,0,1:T(4,128)(2,1)S(1)}, u32[]{:S(2)}, u32[]{:S(2)}) %collective-permute-start) | collective-permute-done | bytes 602144 | tf_op jit(solution)/shard_map/while/body/eval_jaxpr/ppermute | solution.py:14
  91.8 2.6 bitcast_dynamic-update-slice_fusion.4
  95.0 9.2 %collective-permute-start = (bf16[4,196,384]{2,0,1:T(4,128)(2,1)S(1)}, bf16[4,196,384]{2,0,1:T(4,128)(2,1)S(1)}, u32[]{:S(2)}, u32[]{:S(2)}) collective-permute-start(bf16[4,196,384]{2,0,1:T(4,128)(2,1)S(1)} %get-tuple-element.1716), channel_id=1, source_target_pairs={{0,1},{1,2},{2,3},{4,5},{5,6},{6,7},{8,9},{9,10},{10,11},{12,13},{... | collective-permute-start | bytes 1806344 | tf_op jit(solution)/shard_map/while/body/eval_jaxpr/ppermute | solution.py:14
  106.6 7.7 collective-permute-done
  115.6 2.6 bitcast_dynamic-update-slice_fusion.4
  118.8 9.2 %collective-permute-start = (bf16[4,196,384]{2,0,1:T(4,128)(2,1)S(1)}, bf16[4,196,384]{2,0,1:T(4,128)(2,1)S(1)}, u32[]{:S(2)}, u32[]{:S(2)}) collective-permute-start(bf16[4,196,384]{2,0,1:T(4,128)(2,1)S(1)} %get-tuple-element.1716), channel_id=1, source_target_pairs={{0,1},{1,2},{2,3},{4,5},{5,6},{6,7},{8,9},{9,10},{10,11},{12,13},{... | collective-permute-start | bytes 1806344 | tf_op jit(solution)/shard_map/while/body/eval_jaxpr/ppermute | solution.py:14
  130.5 6.7 collective-permute-done
  141.7 9.2 %collective-permute-start = (bf16[4,196,384]{2,0,1:T(4,128)(2,1)S(1)}, bf16[4,196,384]{2,0,1:T(4,128)(2,1)S(1)}, u32[]{:S(2)}, u32[]{:S(2)}) collective-permute-start(bf16[4,196,384]{2,0,1:T(4,128)(2,1)S(1)} %get-tuple-element.1716), channel_id=1, source_target_pairs={{0,1},{1,2},{2,3},{4,5},{5,6},{6,7},{8,9},{9,10},{10,11},{12,13},{... | collective-permute-start | bytes 1806344 | tf_op jit(solution)/shard_map/while/body/eval_jaxpr/ppermute | solution.py:14
  153.4 5.8 collective-permute-done
  163.3 9.7 %collective-permute-start = (bf16[4,196,384]{2,0,1:T(4,128)(2,1)S(1)}, bf16[4,196,384]{2,0,1:T(4,128)(2,1)S(1)}, u32[]{:S(2)}, u32[]{:S(2)}) collective-permute-start(bf16[4,196,384]{2,0,1:T(4,128)(2,1)S(1)} %get-tuple-element.1716), channel_id=1, source_target_pairs={{0,1},{1,2},{2,3},{4,5},{5,6},{6,7},{8,9},{9,10},{10,11},{12,13},{... | collective-permute-start | bytes 1806344 | tf_op jit(solution)/shard_map/while/body/eval_jaxpr/ppermute | solution.py:14
  175.3 5.1 collective-permute-done
  184.5 4.4 collective-permute-start
  191.3 5.1 collective-permute-done
  200.4 4.4 collective-permute-start
  207.3 5.1 collective-permute-done
  212.3 2.7 broadcast.94.clone
  216.1 364.5 %while.56 = (s32[]{:T(128)}, bf16[4,196,384]{2,0,1:T(4,128)(2,1)}, bf16[6,4,196,384]{3,1,2,0:T(4,128)(2,1)}, f32[384]{0:T(512)S(1)}, f32[384]{0:T(512)S(1)}, /*i...) while((s32[]{:T(128)}, bf16[4,196,384]{2,0,1:T(4,128)(2,1)}, ...), condition=%wide.region_18.19_spmd.clone, body=%wide.region_5.18_spmd.clone.sunk | while | flops 5601780224 | bytes 103281600 | solution.py:219
  216.2 4.3 copy.89
  236.6 4.2 collective-permute-done.1
  241.0 4.3 copy.89
  256.7 3.7 select_add_fusion.20
  262.9 6.4 collective-permute-done.1
  269.4 4.3 copy.89
  285.2 3.7 select_add_fusion.20
  291.3 44.8 %collective-permute-done.1 = bf16[4,196,384]{2,0,1:T(4,128)(2,1)} collective-permute-done((bf16[4,196,384]{2,0,1:T(4,128)(2,1)}, bf16[4,196,384]{2,0,1:T(4,128)(2,1)}, u32[]{:S(2)}, u32[]{:S(2)}) %collective-permute-start.1) | collective-permute-done | bytes 602144 | tf_op jit(solution)/shard_map/while/body/eval_jaxpr/ppermute | solution.py:14
  336.3 4.3 copy.89
  345.2 7.7 conditional.6
  357.7 3.7 select_add_fusion.20
  363.9 15.1 %collective-permute-done.1 = bf16[4,196,384]{2,0,1:T(4,128)(2,1)} collective-permute-done((bf16[4,196,384]{2,0,1:T(4,128)(2,1)}, bf16[4,196,384]{2,0,1:T(4,128)(2,1)}, u32[]{:S(2)}, u32[]{:S(2)}) %collective-permute-start.1) | collective-permute-done | bytes 602144 | tf_op jit(solution)/shard_map/while/body/eval_jaxpr/ppermute | solution.py:14
  379.1 4.3 copy.89
  388.1 7.7 conditional.6
  400.5 3.7 select_add_fusion.20
  406.7 15.1 %collective-permute-done.1 = bf16[4,196,384]{2,0,1:T(4,128)(2,1)} collective-permute-done((bf16[4,196,384]{2,0,1:T(4,128)(2,1)}, bf16[4,196,384]{2,0,1:T(4,128)(2,1)}, u32[]{:S(2)}, u32[]{:S(2)}) %collective-permute-start.1) | collective-permute-done | bytes 602144 | tf_op jit(solution)/shard_map/while/body/eval_jaxpr/ppermute | solution.py:14
  422.0 4.3 copy.89
  430.9 7.7 conditional.6
  443.4 3.7 select_add_fusion.20
  449.6 15.1 %collective-permute-done.1 = bf16[4,196,384]{2,0,1:T(4,128)(2,1)} collective-permute-done((bf16[4,196,384]{2,0,1:T(4,128)(2,1)}, bf16[4,196,384]{2,0,1:T(4,128)(2,1)}, u32[]{:S(2)}, u32[]{:S(2)}) %collective-permute-start.1) | collective-permute-done | bytes 602144 | tf_op jit(solution)/shard_map/while/body/eval_jaxpr/ppermute | solution.py:14
  464.8 4.3 copy.89
  473.8 7.7 conditional.6
  486.2 3.7 select_add_fusion.20
  492.4 15.1 %collective-permute-done.1 = bf16[4,196,384]{2,0,1:T(4,128)(2,1)} collective-permute-done((bf16[4,196,384]{2,0,1:T(4,128)(2,1)}, bf16[4,196,384]{2,0,1:T(4,128)(2,1)}, u32[]{:S(2)}, u32[]{:S(2)}) %collective-permute-start.1) | collective-permute-done | bytes 602144 | tf_op jit(solution)/shard_map/while/body/eval_jaxpr/ppermute | solution.py:14
  507.7 4.3 copy.89
  516.6 7.7 conditional.6
  529.1 3.7 select_add_fusion.20
  535.3 15.1 %collective-permute-done.1 = bf16[4,196,384]{2,0,1:T(4,128)(2,1)} collective-permute-done((bf16[4,196,384]{2,0,1:T(4,128)(2,1)}, bf16[4,196,384]{2,0,1:T(4,128)(2,1)}, u32[]{:S(2)}, u32[]{:S(2)}) %collective-permute-start.1) | collective-permute-done | bytes 602144 | tf_op jit(solution)/shard_map/while/body/eval_jaxpr/ppermute | solution.py:14
  550.5 4.3 copy.89
  559.5 7.7 conditional.6
  571.9 3.7 select_add_fusion.20
  580.7 4.4 broadcast_multiply_fusion
  585.1 2.9 broadcast_multiply_fusion.1
  589.3 43.6 %all-reduce = (f32[4,384]{1,0:T(4,128)}, f32[4,384]{1,0:T(4,128)}, f32[4,384]{1,0:T(4,128)}, f32[2,196]{1,0:T(2,128)}, f32[2,1536]{1,0:T(2,128)}, /*index=5*/f32[2,384]{1,0:T(2,128)}) all-reduce(f32[4,384]{1,0:T(4,128)S(1)} %get-tuple-element.1448, ...), channel_id=1, replica_groups=mesh['dp'=8,'section'=4] {'dp','section'}, use_global_device_ids=true, to_apply=%region_19.20 | all-reduce | flops 8840 | bytes 70720 | tf_op jit(solution)/shard_map/psum | solution.py:235
  632.9 153.9 %all-reduce.4.cloned.1.call-done = (f32[2,196,196]{2,0,1:T(2,128)}, f32[2,384,1536]{2,1,0:T(8,128)}, f32[2,1536,384]{2,1,0:T(8,128)}) async-done(((f32[2,196,196]{2,0,1:T(2,128)}, f32[2,384,1536]{2,1,0:T(8,128)}, f32[2,1536,384]{2,1,0:T(8,128)}), (f32[2,196,196]{2,0,1:T(2,128)}, f32[2,384,1536]{2,1,0:T(8,128)}, f32[2,1536,384]{2,1,0:T(8,128)})) %all-reduce.4.cloned.1.call-update) | async-done | bytes 9744528 | tf_op jit(solution)/shard_map/psum | solution.py:235
  788.8 4.9 copy.180
  (597 shorter events, 233.0 us)
Async XLA Ops:
  7.2 779.6 %all-reduce.4.cloned.1.call-start = ((), (), s32[]{:S(2)}) async-start(), calls=%async_computation | async-start | bytes 19677184 | tf_op jit(solution)/shard_map/psum | solution.py:235
  22.8 17.3 %collective-permute-start = (bf16[4,196,384]{2,0,1:T(4,128)(2,1)S(1)}, bf16[4,196,384]{2,0,1:T(4,128)(2,1)S(1)}, u32[]{:S(2)}, u32[]{:S(2)}) collective-permute-start(bf16[4,196,384]{2,0,1:T(4,128)(2,1)S(1)} %get-tuple-element.1716), channel_id=1, source_target_pairs={{0,1},{1,2},{2,3},{4,5},{5,6},{6,7},{8,9},{9,10},{10,11},{12,13},{... | collective-permute-start | bytes 1806344 | tf_op jit(solution)/shard_map/while/body/eval_jaxpr/ppermute | solution.py:14
  44.6 21.1 %collective-permute-start = (bf16[4,196,384]{2,0,1:T(4,128)(2,1)S(1)}, bf16[4,196,384]{2,0,1:T(4,128)(2,1)S(1)}, u32[]{:S(2)}, u32[]{:S(2)}) collective-permute-start(bf16[4,196,384]{2,0,1:T(4,128)(2,1)S(1)} %get-tuple-element.1716), channel_id=1, source_target_pairs={{0,1},{1,2},{2,3},{4,5},{5,6},{6,7},{8,9},{9,10},{10,11},{12,13},{... | collective-permute-start | bytes 1806344 | tf_op jit(solution)/shard_map/while/body/eval_jaxpr/ppermute | solution.py:14
  70.3 20.2 %collective-permute-start = (bf16[4,196,384]{2,0,1:T(4,128)(2,1)S(1)}, bf16[4,196,384]{2,0,1:T(4,128)(2,1)S(1)}, u32[]{:S(2)}, u32[]{:S(2)}) collective-permute-start(bf16[4,196,384]{2,0,1:T(4,128)(2,1)S(1)} %get-tuple-element.1716), channel_id=1, source_target_pairs={{0,1},{1,2},{2,3},{4,5},{5,6},{6,7},{8,9},{9,10},{10,11},{12,13},{... | collective-permute-start | bytes 1806344 | tf_op jit(solution)/shard_map/while/body/eval_jaxpr/ppermute | solution.py:14
  95.0 19.3 %collective-permute-start = (bf16[4,196,384]{2,0,1:T(4,128)(2,1)S(1)}, bf16[4,196,384]{2,0,1:T(4,128)(2,1)S(1)}, u32[]{:S(2)}, u32[]{:S(2)}) collective-permute-start(bf16[4,196,384]{2,0,1:T(4,128)(2,1)S(1)} %get-tuple-element.1716), channel_id=1, source_target_pairs={{0,1},{1,2},{2,3},{4,5},{5,6},{6,7},{8,9},{9,10},{10,11},{12,13},{... | collective-permute-start | bytes 1806344 | tf_op jit(solution)/shard_map/while/body/eval_jaxpr/ppermute | solution.py:14
  118.8 18.4 %collective-permute-start = (bf16[4,196,384]{2,0,1:T(4,128)(2,1)S(1)}, bf16[4,196,384]{2,0,1:T(4,128)(2,1)S(1)}, u32[]{:S(2)}, u32[]{:S(2)}) collective-permute-start(bf16[4,196,384]{2,0,1:T(4,128)(2,1)S(1)} %get-tuple-element.1716), channel_id=1, source_target_pairs={{0,1},{1,2},{2,3},{4,5},{5,6},{6,7},{8,9},{9,10},{10,11},{12,13},{... | collective-permute-start | bytes 1806344 | tf_op jit(solution)/shard_map/while/body/eval_jaxpr/ppermute | solution.py:14
  141.7 17.5 %collective-permute-start = (bf16[4,196,384]{2,0,1:T(4,128)(2,1)S(1)}, bf16[4,196,384]{2,0,1:T(4,128)(2,1)S(1)}, u32[]{:S(2)}, u32[]{:S(2)}) collective-permute-start(bf16[4,196,384]{2,0,1:T(4,128)(2,1)S(1)} %get-tuple-element.1716), channel_id=1, source_target_pairs={{0,1},{1,2},{2,3},{4,5},{5,6},{6,7},{8,9},{9,10},{10,11},{12,13},{... | collective-permute-start | bytes 1806344 | tf_op jit(solution)/shard_map/while/body/eval_jaxpr/ppermute | solution.py:14
  163.3 17.1 %collective-permute-start = (bf16[4,196,384]{2,0,1:T(4,128)(2,1)S(1)}, bf16[4,196,384]{2,0,1:T(4,128)(2,1)S(1)}, u32[]{:S(2)}, u32[]{:S(2)}) collective-permute-start(bf16[4,196,384]{2,0,1:T(4,128)(2,1)S(1)} %get-tuple-element.1716), channel_id=1, source_target_pairs={{0,1},{1,2},{2,3},{4,5},{5,6},{6,7},{8,9},{9,10},{10,11},{12,13},{... | collective-permute-start | bytes 1806344 | tf_op jit(solution)/shard_map/while/body/eval_jaxpr/ppermute | solution.py:14
  184.5 11.9 %collective-permute-start = (bf16[4,196,384]{2,0,1:T(4,128)(2,1)S(1)}, bf16[4,196,384]{2,0,1:T(4,128)(2,1)S(1)}, u32[]{:S(2)}, u32[]{:S(2)}) collective-permute-start(bf16[4,196,384]{2,0,1:T(4,128)(2,1)S(1)} %get-tuple-element.1716), channel_id=1, source_target_pairs={{0,1},{1,2},{2,3},{4,5},{5,6},{6,7},{8,9},{9,10},{10,11},{12,13},{... | collective-permute-start | bytes 1806344 | tf_op jit(solution)/shard_map/while/body/eval_jaxpr/ppermute | solution.py:14
  200.4 11.9 %collective-permute-start = (bf16[4,196,384]{2,0,1:T(4,128)(2,1)S(1)}, bf16[4,196,384]{2,0,1:T(4,128)(2,1)S(1)}, u32[]{:S(2)}, u32[]{:S(2)}) collective-permute-start(bf16[4,196,384]{2,0,1:T(4,128)(2,1)S(1)} %get-tuple-element.1716), channel_id=1, source_target_pairs={{0,1},{1,2},{2,3},{4,5},{5,6},{6,7},{8,9},{9,10},{10,11},{12,13},{... | collective-permute-start | bytes 1806344 | tf_op jit(solution)/shard_map/while/body/eval_jaxpr/ppermute | solution.py:14
  216.1 364.5 %copy-start.11 = (f32[2]{0:T(128)S(1)}, f32[2]{0:T(128)}, u32[]{:S(2)}) copy-start(f32[2]{0:T(128)} %compare_convert_fusion) | copy-start | bytes 28
  228.2 12.7 %collective-permute-start.1 = (bf16[4,196,384]{2,0,1:T(4,128)(2,1)}, bf16[4,196,384]{2,0,1:T(4,128)(2,1)}, u32[]{:S(2)}, u32[]{:S(2)}) collective-permute-start(bf16[4,196,384]{2,0,1:T(4,128)(2,1)} %copy.91), channel_id=1, source_target_pairs={{1,0},{2,1},{3,2},{5,4},{6,5},{7,6},{9,8},{10,9},{11,10},{13,12},{... | collective-permute-start | bytes 1806344 | tf_op jit(solution)/shard_map/while/body/eval_jaxpr/ppermute | solution.py:14
  240.9 9.0 %copy-start.12 = (f32[1536]{0:T(1024)}, f32[1536]{0:T(1024)S(1)}, u32[]{:S(2)}) copy-start(f32[1536]{0:T(1024)S(1)} %get-tuple-element.1950) | copy-start | bytes 18436 | tf_op jit(solution)/shard_map/while
  253.0 16.3 %collective-permute-start.1 = (bf16[4,196,384]{2,0,1:T(4,128)(2,1)}, bf16[4,196,384]{2,0,1:T(4,128)(2,1)}, u32[]{:S(2)}, u32[]{:S(2)}) collective-permute-start(bf16[4,196,384]{2,0,1:T(4,128)(2,1)} %copy.91), channel_id=1, source_target_pairs={{1,0},{2,1},{3,2},{5,4},{6,5},{7,6},{9,8},{10,9},{11,10},{13,12},{... | collective-permute-start | bytes 1806344 | tf_op jit(solution)/shard_map/while/body/eval_jaxpr/ppermute | solution.py:14
  269.3 9.0 %copy-start.12 = (f32[1536]{0:T(1024)}, f32[1536]{0:T(1024)S(1)}, u32[]{:S(2)}) copy-start(f32[1536]{0:T(1024)S(1)} %get-tuple-element.1950) | copy-start | bytes 18436 | tf_op jit(solution)/shard_map/while
  281.4 54.8 %collective-permute-start.1 = (bf16[4,196,384]{2,0,1:T(4,128)(2,1)}, bf16[4,196,384]{2,0,1:T(4,128)(2,1)}, u32[]{:S(2)}, u32[]{:S(2)}) collective-permute-start(bf16[4,196,384]{2,0,1:T(4,128)(2,1)} %copy.91), channel_id=1, source_target_pairs={{1,0},{2,1},{3,2},{5,4},{6,5},{7,6},{9,8},{10,9},{11,10},{13,12},{... | collective-permute-start | bytes 1806344 | tf_op jit(solution)/shard_map/while/body/eval_jaxpr/ppermute | solution.py:14
  289.0 47.2 %copy-start.13 = (f32[1536]{0:T(1024)S(1)}, f32[1536]{0:T(1024)}, u32[]{:S(2)}) copy-start(f32[1536]{0:T(1024)} %copy-done.12) | copy-start | bytes 18436 | tf_op jit(solution)/shard_map/while
  289.0 47.2 %copy-start.16 = (f32[6,4]{1,0:T(8,128)S(1)}, f32[6,4]{1,0:T(8,128)}, u32[]{:S(2)}) copy-start(f32[6,4]{1,0:T(8,128)} %copy-done.15) | copy-start | bytes 292 | tf_op jit(solution)/shard_map/while
  289.0 47.2 %copy-start.19 = (f32[384]{0:T(512)S(1)}, f32[384]{0:T(512)}, u32[]{:S(2)}) copy-start(f32[384]{0:T(512)} %copy-done.18) | copy-start | bytes 4612 | tf_op jit(solution)/shard_map/while
  289.0 47.2 %copy-start.23 = (f32[384]{0:T(512)S(1)}, f32[384]{0:T(512)}, u32[]{:S(2)}) copy-start(f32[384]{0:T(512)} %copy-done.22) | copy-start | bytes 4612 | tf_op jit(solution)/shard_map/while
  289.0 47.2 %copy-start.29 = (f32[196]{0:T(256)S(1)}, f32[196]{0:T(256)}, u32[]{:S(2)}) copy-start(f32[196]{0:T(256)} %copy-done.28) | copy-start | bytes 2356 | tf_op jit(solution)/shard_map/while
  291.3 44.8 %copy-start.4 = (f32[1536,384]{1,0:T(8,128)}, f32[1536,384]{1,0:T(8,128)S(1)}, u32[]{:S(2)}) copy-start(f32[1536,384]{1,0:T(8,128)S(1)} %select_add_fusion.22) | copy-start | bytes 7077892 | tf_op jit(solution)/shard_map/while
  336.2 9.0 %copy-start.12 = (f32[1536]{0:T(1024)}, f32[1536]{0:T(1024)S(1)}, u32[]{:S(2)}) copy-start(f32[1536]{0:T(1024)S(1)} %get-tuple-element.1950) | copy-start | bytes 18436 | tf_op jit(solution)/shard_map/while
  353.9 25.1 %collective-permute-start.1 = (bf16[4,196,384]{2,0,1:T(4,128)(2,1)}, bf16[4,196,384]{2,0,1:T(4,128)(2,1)}, u32[]{:S(2)}, u32[]{:S(2)}) collective-permute-start(bf16[4,196,384]{2,0,1:T(4,128)(2,1)} %copy.91), channel_id=1, source_target_pairs={{1,0},{2,1},{3,2},{5,4},{6,5},{7,6},{9,8},{10,9},{11,10},{13,12},{... | collective-permute-start | bytes 1806344 | tf_op jit(solution)/shard_map/while/body/eval_jaxpr/ppermute | solution.py:14
  361.5 17.5 %copy-start.13 = (f32[1536]{0:T(1024)S(1)}, f32[1536]{0:T(1024)}, u32[]{:S(2)}) copy-start(f32[1536]{0:T(1024)} %copy-done.12) | copy-start | bytes 18436 | tf_op jit(solution)/shard_map/while
  361.5 17.5 %copy-start.16 = (f32[6,4]{1,0:T(8,128)S(1)}, f32[6,4]{1,0:T(8,128)}, u32[]{:S(2)}) copy-start(f32[6,4]{1,0:T(8,128)} %copy-done.15) | copy-start | bytes 292 | tf_op jit(solution)/shard_map/while
  361.5 17.5 %copy-start.19 = (f32[384]{0:T(512)S(1)}, f32[384]{0:T(512)}, u32[]{:S(2)}) copy-start(f32[384]{0:T(512)} %copy-done.18) | copy-start | bytes 4612 | tf_op jit(solution)/shard_map/while
  361.5 17.5 %copy-start.23 = (f32[384]{0:T(512)S(1)}, f32[384]{0:T(512)}, u32[]{:S(2)}) copy-start(f32[384]{0:T(512)} %copy-done.22) | copy-start | bytes 4612 | tf_op jit(solution)/shard_map/while
  361.5 17.5 %copy-start.29 = (f32[196]{0:T(256)S(1)}, f32[196]{0:T(256)}, u32[]{:S(2)}) copy-start(f32[196]{0:T(256)} %copy-done.28) | copy-start | bytes 2356 | tf_op jit(solution)/shard_map/while
  363.9 15.1 %copy-start.4 = (f32[1536,384]{1,0:T(8,128)}, f32[1536,384]{1,0:T(8,128)S(1)}, u32[]{:S(2)}) copy-start(f32[1536,384]{1,0:T(8,128)S(1)} %select_add_fusion.22) | copy-start | bytes 7077892 | tf_op jit(solution)/shard_map/while
  379.1 9.0 %copy-start.12 = (f32[1536]{0:T(1024)}, f32[1536]{0:T(1024)S(1)}, u32[]{:S(2)}) copy-start(f32[1536]{0:T(1024)S(1)} %get-tuple-element.1950) | copy-start | bytes 18436 | tf_op jit(solution)/shard_map/while
  396.8 25.1 %collective-permute-start.1 = (bf16[4,196,384]{2,0,1:T(4,128)(2,1)}, bf16[4,196,384]{2,0,1:T(4,128)(2,1)}, u32[]{:S(2)}, u32[]{:S(2)}) collective-permute-start(bf16[4,196,384]{2,0,1:T(4,128)(2,1)} %copy.91), channel_id=1, source_target_pairs={{1,0},{2,1},{3,2},{5,4},{6,5},{7,6},{9,8},{10,9},{11,10},{13,12},{... | collective-permute-start | bytes 1806344 | tf_op jit(solution)/shard_map/while/body/eval_jaxpr/ppermute | solution.py:14
  404.3 17.5 %copy-start.13 = (f32[1536]{0:T(1024)S(1)}, f32[1536]{0:T(1024)}, u32[]{:S(2)}) copy-start(f32[1536]{0:T(1024)} %copy-done.12) | copy-start | bytes 18436 | tf_op jit(solution)/shard_map/while
  404.4 17.5 %copy-start.16 = (f32[6,4]{1,0:T(8,128)S(1)}, f32[6,4]{1,0:T(8,128)}, u32[]{:S(2)}) copy-start(f32[6,4]{1,0:T(8,128)} %copy-done.15) | copy-start | bytes 292 | tf_op jit(solution)/shard_map/while
  404.4 17.5 %copy-start.19 = (f32[384]{0:T(512)S(1)}, f32[384]{0:T(512)}, u32[]{:S(2)}) copy-start(f32[384]{0:T(512)} %copy-done.18) | copy-start | bytes 4612 | tf_op jit(solution)/shard_map/while
  404.4 17.5 %copy-start.23 = (f32[384]{0:T(512)S(1)}, f32[384]{0:T(512)}, u32[]{:S(2)}) copy-start(f32[384]{0:T(512)} %copy-done.22) | copy-start | bytes 4612 | tf_op jit(solution)/shard_map/while
  404.4 17.5 %copy-start.29 = (f32[196]{0:T(256)S(1)}, f32[196]{0:T(256)}, u32[]{:S(2)}) copy-start(f32[196]{0:T(256)} %copy-done.28) | copy-start | bytes 2356 | tf_op jit(solution)/shard_map/while
  406.7 15.1 %copy-start.4 = (f32[1536,384]{1,0:T(8,128)}, f32[1536,384]{1,0:T(8,128)S(1)}, u32[]{:S(2)}) copy-start(f32[1536,384]{1,0:T(8,128)S(1)} %select_add_fusion.22) | copy-start | bytes 7077892 | tf_op jit(solution)/shard_map/while
  421.9 9.0 %copy-start.12 = (f32[1536]{0:T(1024)}, f32[1536]{0:T(1024)S(1)}, u32[]{:S(2)}) copy-start(f32[1536]{0:T(1024)S(1)} %get-tuple-element.1950) | copy-start | bytes 18436 | tf_op jit(solution)/shard_map/while
  439.6 25.1 %collective-permute-start.1 = (bf16[4,196,384]{2,0,1:T(4,128)(2,1)}, bf16[4,196,384]{2,0,1:T(4,128)(2,1)}, u32[]{:S(2)}, u32[]{:S(2)}) collective-permute-start(bf16[4,196,384]{2,0,1:T(4,128)(2,1)} %copy.91), channel_id=1, source_target_pairs={{1,0},{2,1},{3,2},{5,4},{6,5},{7,6},{9,8},{10,9},{11,10},{13,12},{... | collective-permute-start | bytes 1806344 | tf_op jit(solution)/shard_map/while/body/eval_jaxpr/ppermute | solution.py:14
  447.2 17.5 %copy-start.13 = (f32[1536]{0:T(1024)S(1)}, f32[1536]{0:T(1024)}, u32[]{:S(2)}) copy-start(f32[1536]{0:T(1024)} %copy-done.12) | copy-start | bytes 18436 | tf_op jit(solution)/shard_map/while
  447.2 17.5 %copy-start.16 = (f32[6,4]{1,0:T(8,128)S(1)}, f32[6,4]{1,0:T(8,128)}, u32[]{:S(2)}) copy-start(f32[6,4]{1,0:T(8,128)} %copy-done.15) | copy-start | bytes 292 | tf_op jit(solution)/shard_map/while
  447.2 17.5 %copy-start.19 = (f32[384]{0:T(512)S(1)}, f32[384]{0:T(512)}, u32[]{:S(2)}) copy-start(f32[384]{0:T(512)} %copy-done.18) | copy-start | bytes 4612 | tf_op jit(solution)/shard_map/while
  447.2 17.5 %copy-start.23 = (f32[384]{0:T(512)S(1)}, f32[384]{0:T(512)}, u32[]{:S(2)}) copy-start(f32[384]{0:T(512)} %copy-done.22) | copy-start | bytes 4612 | tf_op jit(solution)/shard_map/while
  447.2 17.5 %copy-start.29 = (f32[196]{0:T(256)S(1)}, f32[196]{0:T(256)}, u32[]{:S(2)}) copy-start(f32[196]{0:T(256)} %copy-done.28) | copy-start | bytes 2356 | tf_op jit(solution)/shard_map/while
  449.6 15.1 %copy-start.4 = (f32[1536,384]{1,0:T(8,128)}, f32[1536,384]{1,0:T(8,128)S(1)}, u32[]{:S(2)}) copy-start(f32[1536,384]{1,0:T(8,128)S(1)} %select_add_fusion.22) | copy-start | bytes 7077892 | tf_op jit(solution)/shard_map/while
  464.8 9.0 %copy-start.12 = (f32[1536]{0:T(1024)}, f32[1536]{0:T(1024)S(1)}, u32[]{:S(2)}) copy-start(f32[1536]{0:T(1024)S(1)} %get-tuple-element.1950) | copy-start | bytes 18436 | tf_op jit(solution)/shard_map/while
  482.5 25.1 %collective-permute-start.1 = (bf16[4,196,384]{2,0,1:T(4,128)(2,1)}, bf16[4,196,384]{2,0,1:T(4,128)(2,1)}, u32[]{:S(2)}, u32[]{:S(2)}) collective-permute-start(bf16[4,196,384]{2,0,1:T(4,128)(2,1)} %copy.91), channel_id=1, source_target_pairs={{1,0},{2,1},{3,2},{5,4},{6,5},{7,6},{9,8},{10,9},{11,10},{13,12},{... | collective-permute-start | bytes 1806344 | tf_op jit(solution)/shard_map/while/body/eval_jaxpr/ppermute | solution.py:14
  490.0 17.5 %copy-start.13 = (f32[1536]{0:T(1024)S(1)}, f32[1536]{0:T(1024)}, u32[]{:S(2)}) copy-start(f32[1536]{0:T(1024)} %copy-done.12) | copy-start | bytes 18436 | tf_op jit(solution)/shard_map/while
  490.1 17.5 %copy-start.16 = (f32[6,4]{1,0:T(8,128)S(1)}, f32[6,4]{1,0:T(8,128)}, u32[]{:S(2)}) copy-start(f32[6,4]{1,0:T(8,128)} %copy-done.15) | copy-start | bytes 292 | tf_op jit(solution)/shard_map/while
  490.1 17.5 %copy-start.19 = (f32[384]{0:T(512)S(1)}, f32[384]{0:T(512)}, u32[]{:S(2)}) copy-start(f32[384]{0:T(512)} %copy-done.18) | copy-start | bytes 4612 | tf_op jit(solution)/shard_map/while
  490.1 17.5 %copy-start.23 = (f32[384]{0:T(512)S(1)}, f32[384]{0:T(512)}, u32[]{:S(2)}) copy-start(f32[384]{0:T(512)} %copy-done.22) | copy-start | bytes 4612 | tf_op jit(solution)/shard_map/while
  490.1 17.5 %copy-start.29 = (f32[196]{0:T(256)S(1)}, f32[196]{0:T(256)}, u32[]{:S(2)}) copy-start(f32[196]{0:T(256)} %copy-done.28) | copy-start | bytes 2356 | tf_op jit(solution)/shard_map/while
  492.4 15.1 %copy-start.4 = (f32[1536,384]{1,0:T(8,128)}, f32[1536,384]{1,0:T(8,128)S(1)}, u32[]{:S(2)}) copy-start(f32[1536,384]{1,0:T(8,128)S(1)} %select_add_fusion.22) | copy-start | bytes 7077892 | tf_op jit(solution)/shard_map/while
  507.6 9.0 %copy-start.12 = (f32[1536]{0:T(1024)}, f32[1536]{0:T(1024)S(1)}, u32[]{:S(2)}) copy-start(f32[1536]{0:T(1024)S(1)} %get-tuple-element.1950) | copy-start | bytes 18436 | tf_op jit(solution)/shard_map/while
  525.3 25.1 %collective-permute-start.1 = (bf16[4,196,384]{2,0,1:T(4,128)(2,1)}, bf16[4,196,384]{2,0,1:T(4,128)(2,1)}, u32[]{:S(2)}, u32[]{:S(2)}) collective-permute-start(bf16[4,196,384]{2,0,1:T(4,128)(2,1)} %copy.91), channel_id=1, source_target_pairs={{1,0},{2,1},{3,2},{5,4},{6,5},{7,6},{9,8},{10,9},{11,10},{13,12},{... | collective-permute-start | bytes 1806344 | tf_op jit(solution)/shard_map/while/body/eval_jaxpr/ppermute | solution.py:14
  532.9 17.5 %copy-start.13 = (f32[1536]{0:T(1024)S(1)}, f32[1536]{0:T(1024)}, u32[]{:S(2)}) copy-start(f32[1536]{0:T(1024)} %copy-done.12) | copy-start | bytes 18436 | tf_op jit(solution)/shard_map/while
  532.9 17.5 %copy-start.16 = (f32[6,4]{1,0:T(8,128)S(1)}, f32[6,4]{1,0:T(8,128)}, u32[]{:S(2)}) copy-start(f32[6,4]{1,0:T(8,128)} %copy-done.15) | copy-start | bytes 292 | tf_op jit(solution)/shard_map/while
  532.9 17.5 %copy-start.19 = (f32[384]{0:T(512)S(1)}, f32[384]{0:T(512)}, u32[]{:S(2)}) copy-start(f32[384]{0:T(512)} %copy-done.18) | copy-start | bytes 4612 | tf_op jit(solution)/shard_map/while
  532.9 17.5 %copy-start.23 = (f32[384]{0:T(512)S(1)}, f32[384]{0:T(512)}, u32[]{:S(2)}) copy-start(f32[384]{0:T(512)} %copy-done.22) | copy-start | bytes 4612 | tf_op jit(solution)/shard_map/while
  532.9 17.5 %copy-start.29 = (f32[196]{0:T(256)S(1)}, f32[196]{0:T(256)}, u32[]{:S(2)}) copy-start(f32[196]{0:T(256)} %copy-done.28) | copy-start | bytes 2356 | tf_op jit(solution)/shard_map/while
  535.3 15.1 %copy-start.4 = (f32[1536,384]{1,0:T(8,128)}, f32[1536,384]{1,0:T(8,128)S(1)}, u32[]{:S(2)}) copy-start(f32[1536,384]{1,0:T(8,128)S(1)} %select_add_fusion.22) | copy-start | bytes 7077892 | tf_op jit(solution)/shard_map/while
  550.5 9.0 %copy-start.12 = (f32[1536]{0:T(1024)}, f32[1536]{0:T(1024)S(1)}, u32[]{:S(2)}) copy-start(f32[1536]{0:T(1024)S(1)} %get-tuple-element.1950) | copy-start | bytes 18436 | tf_op jit(solution)/shard_map/while
  568.2 12.2 %collective-permute-start.1 = (bf16[4,196,384]{2,0,1:T(4,128)(2,1)}, bf16[4,196,384]{2,0,1:T(4,128)(2,1)}, u32[]{:S(2)}, u32[]{:S(2)}) collective-permute-start(bf16[4,196,384]{2,0,1:T(4,128)(2,1)} %copy.91), channel_id=1, source_target_pairs={{1,0},{2,1},{3,2},{5,4},{6,5},{7,6},{9,8},{10,9},{11,10},{13,12},{... | collective-permute-start | bytes 1806344 | tf_op jit(solution)/shard_map/while/body/eval_jaxpr/ppermute | solution.py:14
  (96 other events, 518.1 us)
Sparse Core Ops, SparseCore 0:
  589.1 197.6 all-reduce.3
where the time goes:
time: 809 us; the launch traced here: 804 us
  waiting for transfers between devices  351 us (43%)
  local copies, waits for them, and re-layouts  160 us (20%)
  other arithmetic  119 us (15%)
  starting transfers between devices  80.6 us (10%)
  blocking collectives  43.6 us (5%)
  matrix products  32.5 us (4%)
  between operations  14.3 us (2%)
    ppermute x18, waiting for transfers between devices, from_behind(): lax.ppermute(value, axis, [(source, source + steps) for source in range(i...  197 us
    psum x1, waiting for transfers between devices, shards(): lax.psum((on_section * g_alpha, on_section * g_beta, on_section * g_gain,...  154 us
    ppermute x18, starting transfers between devices, from_behind(): lax.ppermute(value, axis, [(source, source + steps) for source in range(i...  80.5 us
    add x63, other arithmetic, backward_tick(): totals = jax.tree.map(lambda left, right: left + right, totals, grads)  52.8 us
    psum x1, blocking collectives, shards(): lax.psum((on_section * g_alpha, on_section * g_beta, on_section * g_gain,...  43.6 us
    while x225, local copies, waits for them, and re-layouts  40 us
    dynamic_update_slice x9, other arithmetic, forward_tick(): lax.dynamic_update_index_in_dim(kept, jnp.where(valid, xin, kept[slot]),...  23.3 us
    select_n x9, other arithmetic, backward_tick(): gout = jnp.where(section == n_section - 1, fresh, incoming)  21.1 us
  transfers between devices with their start and end apart: 19, of which 19 were waited for; matrix products, arithmetic and copies ran while one was open for 12% of the time, Pallas kernels for 0%

commit v1 on v0

v1 whole, which is shorter than its diff:
```python
import functools

import jax
import jax.numpy as jnp
from jax import lax
from jax.experimental import pallas as pl
from jax.experimental.pallas import tpu as pltpu
from jax.sharding import PartitionSpec as P

f32, bf16 = jnp.float32, jnp.bfloat16
C0 = 0.7978845608028654
C1 = 0.044715
SMALL_ROWS = 12
ROW_SCALE, ROW_SHIFT, ROW_GAIN, ROW_OFFSET, ROW_UPB = 0, 2, 4, 6, 7


def dot(a, b, ca=1, cb=0):
    return lax.dot_general(a, b, (((ca,), (cb,)), ((), ())), preferred_element_type=f32)


def up_to(n, k):
    return -(-n // k) * k


def gelu_parts(pre):
    pre = pre.astype(bf16)
    c0, c01, c03 = bf16(C0), bf16(C0 * C1), bf16(3 * C0 * C1)
    half, one = bf16(0.5), bf16(1.0)
    square = pre * pre
    t = jnp.tanh(pre * (c0 + c01 * square))
    hx = half * pre
    return hx + hx * t, (half + half * t) + hx * (one - t * t) * (c0 + c03 * square)


def plan(sec, t, M):
    half = M // 2
    mine = t < half
    m = lax.rem(t + half * lax.rem(sec, 2), M)
    yes = sec >= 0
    return dict(
        m=m, mine=mine, ffn0=yes, patch1=yes, up1=yes, down1=sec == 3,
        back_ffn1=yes, back_patch1=(sec < 3) | mine, back_ffn0=sec < 2, back_patch0=(sec == 0) | ((sec == 1) & mine),
    )


def compute_kernel(NC, RC, get_sec, live_ref, img_h, og_h, ac, sh, ls, pw_in, pb_in, wu_h, bu, wd_h, bd, out_h, gin_h, grad_o,
                   img, og, outs, gins, wu, wd, pw, rs, kk, aa, bdl, wus, wds, bus, stage, xw, xt, gw, gt, hid, slope, dpre,
                   gx, gd, gp, gsum, sd, bup, gdn, in_sem, out_sem, w_sem):
    M, P, B, D = img.shape
    L, _, H = wu.shape
    PP = pw.shape[1]
    R = B * PP
    sec = get_sec()
    own = sec // 2

    def rows(b):
        return slice(b * PP, (b + 1) * PP)

    def cols(b):
        return slice(b * D, (b + 1) * D)

    def vec(ref, k):
        return ref[k:k + 1, :].astype(f32)

    def load(t, which):
        m = plan(sec, t, M)["m"]
        return pltpu.make_async_copy((img_h, og_h)[which].at[m], (img, og)[which].at[m], in_sem.at[which, m])

    load(0, 0).start()
    w_up = pltpu.make_async_copy(wu_h, wu, w_sem.at[0])
    w_down = pltpu.make_async_copy(wd_h, wd, w_sem.at[1])
    w_up.start()
    w_down.start()
    load(0, 1).start()
    for t in range(1, M):
        load(t, 0).start()
        load(t, 1).start()

    pw[...] = jnp.zeros_like(pw)
    pbt = jnp.concatenate([pb_in[...].astype(f32), jnp.zeros((8 - L, P), f32)], axis=0).T
    stage[...] = jnp.zeros_like(stage)
    for l in range(L):
        pw[l, :P, :P] = pw_in[:, l, :]
        rs[l] = jnp.sum(pw[l].astype(f32), axis=1, keepdims=True)
        stage[0:P, l:l + 1] = pbt[:, l:l + 1]
        kk[l] = vec(ls, 2 * l) * (vec(sh, 2 * l) * rs[l] + stage[0:PP, l:l + 1])
        aa[l] = vec(ac, 2 * l) * vec(ls, 2 * l)
        bdl[l] = vec(bd, l) * vec(ls, 2 * l + 1)
    stage[0:PP, 0:128] = jnp.zeros((PP, 128), f32)
    for r in (gx, gd, gp, gsum, sd, bup, gdn):
        r[...] = jnp.zeros_like(r)
    w_up.wait()
    w_down.wait()
    for l in range(L):
        acol = jnp.broadcast_to(vec(ac, 2 * l + 1), (8, D)).T[:, 0:1]
        shift8 = jnp.broadcast_to(vec(sh, 2 * l + 1), (8, D)).astype(bf16)
        for k in range(0, H, D):
            wus[l, :, k:k + D] = (wu[l, :, k:k + D].astype(f32) * acol).astype(bf16)
            wds[l, k:k + D, :] = (wd[l, k:k + D, :].astype(f32) * vec(ls, 2 * l + 1)).astype(bf16)
            bus[l, :, k:k + D] = dot(shift8, wu[l, :, k:k + D])[0:1, :] + bu[l:l + 1, k:k + D].astype(f32)

    def take(ref, m):
        v = jnp.swapaxes(ref[m].astype(f32), 0, 1)
        for b in range(B):
            stage[b * PP:b * PP + P, :] = v[b] * live_ref[b, m].astype(f32)
            stage[b * PP + P:(b + 1) * PP, :] = jnp.zeros((PP - P, D), f32)

    def give(which, m, pieces):
        v = jnp.stack([p[0:P, :] for p in pieces], axis=0)
        (outs, gins)[which][m] = jnp.swapaxes(v, 0, 1).astype(bf16)
        pltpu.make_async_copy((outs, gins)[which].at[m], (out_h, gin_h)[which].at[m], out_sem.at[which, m]).start()

    def chunk(c):
        return pl.ds(pl.multiple_of(c * NC, NC), NC)

    def row_chunk(r):
        return pl.ds(pl.multiple_of(r * RC, RC), RC)

    def step(t, carry):
        p = plan(sec, t, M)
        m = p["m"]
        load(t, 0).wait()
        take(img, m)
        for b in range(B):
            xw[0, :, cols(b)] = stage[rows(b), :].astype(bf16)

        def forward(l, carry):
            @pl.when((l == 0) | p["patch1"])
            def _():
                mix = dot(pw[l], xw[l])
                new = [xw[l, :, cols(b)].astype(f32) + (aa[l] * mix[:, cols(b)] + kk[l]) for b in range(B)]
                xt[l] = jnp.concatenate(new, axis=0).astype(bf16)

                @pl.when(sec == 2 * l)
                def _():
                    give(0, m, new)

            @pl.when(jnp.where(l == 0, p["ffn0"], p["up1"]))
            def _():
                def up(c, carry):
                    pre = dot(xt[l], wus[l, :, chunk(c)]) + bus[l, :, chunk(c)]
                    h, s = gelu_parts(pre)
                    hid[l, :, chunk(c)] = h
                    slope[l, :, chunk(c)] = s
                    return carry
                lax.fori_loop(0, H // NC, up, 0)

            @pl.when(jnp.where(l == 0, p["ffn0"], p["down1"]))
            def _():
                def down(r, carry):
                    q = row_chunk(r)
                    stage[q, :] = xt[l, q, :].astype(f32) + (dot(hid[l, q, :], wds[l]) + bdl[l])
                    return carry
                lax.fori_loop(0, R // RC, down, 0)

                @pl.when(l + 1 < L)
                def _():
                    for b in range(B):
                        xw[l + 1, :, cols(b)] = stage[rows(b), :].astype(bf16)

                @pl.when(sec == 2 * l + 1)
                def _():
                    give(0, m, [stage[rows(b), :] for b in range(B)])
            return carry

        lax.fori_loop(0, L, forward, 0)

        load(t, 1).wait()

        @pl.when(p["back_ffn1"])
        def _():
            take(og, m)
            gt[...] = stage[...].astype(bf16)

        def backward(i, carry):
            l = L - 1 - i
            weights = p["mine"] & (own == l)

            @pl.when(jnp.where(l == 0, p["back_ffn0"], p["back_ffn1"]))
            def _():
                def dh(c, carry):
                    d = dot(gt[...], wds[l, chunk(c), :], 1, 1)
                    dpre[:, chunk(c)] = (d * slope[l, :, chunk(c)].astype(f32)).astype(bf16)
                    return carry
                lax.fori_loop(0, H // NC, dh, 0)

                def du(r, carry):
                    q = row_chunk(r)
                    stage[q, :] = gt[q, :].astype(f32) + dot(dpre[q, :], wus[l], 1, 1)
                    return carry
                lax.fori_loop(0, R // RC, du, 0)

                @pl.when(weights)
                def _():
                    gdn[...] += jnp.sum(gt[...].astype(f32), axis=0, keepdims=True)
                    g_t = gt[...].T
                    x_t = xt[l].T

                    def grads(c, carry):
                        q = chunk(c)
                        d = dpre[:, q]
                        gx[:, q] += dot(x_t, d)
                        gd[:, q] += dot(g_t, hid[l, :, q])
                        bup[:, q] += jnp.sum(d.astype(f32), axis=0, keepdims=True)
                        return carry
                    lax.fori_loop(0, H // NC, grads, 0)
                for b in range(B):
                    gw[:, cols(b)] = stage[rows(b), :].astype(bf16)

                @pl.when(sec == 2 * l + 1)
                def _():
                    give(1, m, [stage[rows(b), :] for b in range(B)])

            @pl.when(jnp.where(l == 0, p["back_patch0"], p["back_patch1"]))
            def _():
                back = dot(pw[l], gw[...], 0, 0)
                new = [gw[:, cols(b)].astype(f32) + aa[l] * back[:, cols(b)] for b in range(B)]
                gt[...] = jnp.concatenate(new, axis=0).astype(bf16)

                @pl.when(sec == 2 * l)
                def _():
                    give(1, m, new)

                @pl.when(weights)
                def _():
                    scaled = jnp.concatenate([(gw[:, cols(b)].astype(f32) * aa[l]).astype(bf16) for b in range(B)], axis=1)
                    gp[...] += dot(scaled, xw[l], 1, 1)
                    for b in range(B):
                        gsum[...] += gw[:, cols(b)].astype(f32)
                        sd[...] += jnp.sum(back[:, cols(b)] * xw[l, :, cols(b)].astype(f32), axis=0, keepdims=True)
            return carry

        lax.fori_loop(0, L, backward, 0)
        return carry

    lax.fori_loop(0, M, step, 0)

    for l in range(L):
        @pl.when(own == l)
        def _():
            acol = jnp.broadcast_to(vec(ac, 2 * l + 1), (8, D)).T[:, 0:1]
            ccol = jnp.broadcast_to(vec(sh, 2 * l + 1), (8, D)).T[:, 0:1]
            scale1 = jnp.zeros((D, 1), f32)
            shift1 = jnp.zeros((D, 1), f32)
            for k in range(0, H, D):
                g = gx[:, k:k + D]
                w = wu[l, :, k:k + D].astype(f32)
                b = bup[:, k:k + D]
                grad_o[k:k + D, :] = (acol * g + ccol * b).astype(bf16)
                scale1 += jnp.sum(w * g, axis=1, keepdims=True)
                shift1 += jnp.sum(w * b, axis=1, keepdims=True)
            gain1 = vec(bd, l) * gdn[...]
            for k in range(0, H, D):
                g = gd[:, k:k + D].T
                gain1 += jnp.sum(g * wd[l, k:k + D, :].astype(f32), axis=0, keepdims=True)
                grad_o[H + k:H + k + D, :] = (g * vec(ls, 2 * l + 1)).astype(bf16)
            both = jnp.broadcast_to(jnp.concatenate([scale1, shift1], axis=1), (D, 2)).T
            gs = gsum[...]
            lsrow, crow = vec(ls, 2 * l), vec(sh, 2 * l)
            wsum = jnp.sum(gs * rs[l], axis=0, keepdims=True)
            stage[0:PP, 0:PP] = gp[...] + jnp.sum(gs * (lsrow * crow), axis=1, keepdims=True)
            stage[0:PP, 256:257] = jnp.zeros((PP, 1), f32)
            stage[0:P, 256:257] = pbt[:, l:l + 1]
            psum = jnp.sum(gs * stage[0:PP, 256:257], axis=0, keepdims=True)
            offset = jnp.broadcast_to(jnp.sum(gs * lsrow, axis=1, keepdims=True), (PP, 8)).T[0:1, :]
            s_row = sd[...]
            extra = P + SMALL_ROWS

            def put(k, row):
                stage[P + k:P + k + 1, 0:row.shape[1]] = row
            stage[P:extra, :] = jnp.zeros((SMALL_ROWS, D), f32)
            put(ROW_SCALE, lsrow * s_row)
            put(ROW_SCALE + 1, both[0:1, :])
            put(ROW_SHIFT, lsrow * wsum)
            put(ROW_SHIFT + 1, both[1:2, :])
            put(ROW_GAIN, vec(ac, 2 * l) * s_row + crow * wsum + psum)
            put(ROW_GAIN + 1, gain1)
            put(ROW_OFFSET, offset[:, 0:P])
            for k in range(H // D):
                put(ROW_UPB + k, bup[:, k * D:(k + 1) * D])
            put(ROW_UPB + H // D, vec(ls, 2 * l + 1) * gdn[...])
            grad_o[2 * H:2 * H + extra, :] = stage[0:extra, :].astype(bf16)
    grad_o[2 * H + P + SMALL_ROWS:, :] = jnp.zeros((grad_o.shape[0] - 2 * H - P - SMALL_ROWS, D), bf16)
    for m in range(M):
        for which in range(2):
            pltpu.make_async_copy((outs, gins)[which].at[m], (out_h, gin_h)[which].at[m], out_sem.at[which, m]).wait()


def compute_call(get_sec, grad_rows, images, out_grad, live, ac, sh, ls, pw, pb, wu, bu, wd, bd, NC=1536, RC=800):
    M, P, B, D = images.shape
    L, _, H = wu.shape
    PP = up_to(P, 8)
    R = B * PP
    vm = pl.BlockSpec(memory_space=pltpu.VMEM)
    hbm = pl.BlockSpec(memory_space=pl.ANY)
    return pl.pallas_call(
        functools.partial(compute_kernel, NC, RC, get_sec),
        in_specs=[pl.BlockSpec(memory_space=pltpu.SMEM), hbm, hbm, vm, vm, vm, vm, vm, hbm, vm, hbm, vm],
        out_specs=[hbm, hbm, vm],
        out_shape=[jax.ShapeDtypeStruct(images.shape, bf16)] * 2 + [jax.ShapeDtypeStruct((grad_rows, D), bf16)],
        scratch_shapes=[
            pltpu.VMEM(images.shape, bf16), pltpu.VMEM(images.shape, bf16), pltpu.VMEM(images.shape, bf16), pltpu.VMEM(images.shape, bf16),
            pltpu.VMEM((L, D, H), bf16), pltpu.VMEM((L, H, D), bf16),
            pltpu.VMEM((L, PP, PP), bf16), pltpu.VMEM((L, PP, 1), f32), pltpu.VMEM((L, PP, D), f32), pltpu.VMEM((L, 1, D), f32), pltpu.VMEM((L, 1, D), f32),
            pltpu.VMEM((L, D, H), bf16), pltpu.VMEM((L, H, D), bf16), pltpu.VMEM((L, 1, H), f32),
            pltpu.VMEM((R, D), f32),
            pltpu.VMEM((L, PP, B * D), bf16), pltpu.VMEM((L, R, D), bf16), pltpu.VMEM((PP, B * D), bf16), pltpu.VMEM((R, D), bf16),
            pltpu.VMEM((L, R, H), bf16), pltpu.VMEM((L, R, H), bf16), pltpu.VMEM((R, H), bf16),
            pltpu.VMEM((D, H), f32), pltpu.VMEM((D, H), f32), pltpu.VMEM((PP, PP), f32), pltpu.VMEM((PP, D), f32),
            pltpu.VMEM((1, D), f32), pltpu.VMEM((1, H), f32), pltpu.VMEM((1, D), f32),
            pltpu.SemaphoreType.DMA((2, M)), pltpu.SemaphoreType.DMA((2, M)), pltpu.SemaphoreType.DMA((2,)),
        ],
        compiler_params=pltpu.CompilerParams(vmem_limit_bytes=60 * 2**20),
        name="chain",
    )(live, images, out_grad, ac, sh, ls, pw, pb, wu, bu, wd, bd)


def bits_of(n):
    return n.bit_length() - 1


def reduce_unit(n_dp):
    return 16 * n_dp


def reduce_kernel(n_dp, n_sec, g_ref, full, work, recv, send_sem, recv_sem, z_send, z_recv, g_send, g_recv):
    nb = bits_of(n_dp)
    half = full.shape[1] // 2
    unit = reduce_unit(n_dp)
    part_a = up_half = -(-(half // unit) // 2) * unit
    parts = [(0, part_a), (part_a, half - part_a)]
    parts = [p for p in parts if p[1] > 0]
    me = lax.axis_index("dp")
    sec = lax.axis_index("section")
    layer = sec // 2
    rest = list(range(1, nb))
    orders = [rest, rest[::-1]]
    bit = [(me // (1 << j)) % 2 for j in range(nb)]
    zbit = sec % 2

    def peer(j):
        return (me + (1 << j) - 2 * (1 << j) * bit[j], sec)

    zpeer = (me, sec + 1 - 2 * zbit)

    barrier = pltpu.get_barrier_semaphore()
    for j in range(nb):
        pl.semaphore_signal(barrier, inc=1, device_id=peer(j), device_id_type=pl.DeviceIdType.MESH)

    @pl.when(sec > 0)
    def _():
        pl.semaphore_signal(barrier, inc=1, device_id=(me, sec - 1), device_id_type=pl.DeviceIdType.MESH)

    @pl.when(sec < n_sec - 1)
    def _():
        pl.semaphore_signal(barrier, inc=1, device_id=(me, sec + 1), device_id_type=pl.DeviceIdType.MESH)

    pl.semaphore_wait(barrier, nb + jnp.where(sec > 0, 1, 0) + jnp.where(sec < n_sec - 1, 1, 0))

    def copy(src, dst, s, r, device):
        return pltpu.make_async_remote_copy(src_ref=src, dst_ref=dst, send_sem=s, recv_sem=r, device_id=device, device_id_type=pl.DeviceIdType.MESH)

    def rows(off, n):
        return pl.ds(pl.multiple_of(off, 16), n)

    base = bit[0] * half
    first = copy(g_ref.at[rows((1 - bit[0]) * half, half)], recv.at[pl.ds(0, half)], send_sem.at[0, 0], recv_sem.at[0, 0], peer(0))
    first.start()
    first.wait()
    work[...] = (g_ref[rows(base, half), :].astype(f32) + recv[0:half, :].astype(f32)).astype(bf16)

    place = [jnp.int32(off) for off, _ in parts]
    size = [n for _, n in parts]
    slot = half
    for t in range(nb):
        pending = []
        for k in range(len(parts)):
            n = size[k] // 2
            if t < nb - 1:
                b, device = bit[orders[k][t]], peer(orders[k][t])
            else:
                b, device = zbit, zpeer
            c = copy(work.at[rows(place[k] + (1 - b) * n, n)], recv.at[pl.ds(slot, n)], send_sem.at[k, t + 1], recv_sem.at[k, t + 1], device)
            c.start()
            pending.append((c, place[k] + b * n, n, slot))
            slot += n
        for k, (c, keep, n, at) in enumerate(pending):
            c.wait()
            total = work[rows(keep, n), :].astype(f32) + recv[at:at + n, :].astype(f32)
            if t < nb - 1:
                work[rows(keep, n), :] = total.astype(bf16)
            else:
                full[layer, rows(base + keep, n), :] = total.astype(bf16)
            place[k], size[k] = keep, n

    def piece(k, j):
        return full.at[j // 2, rows(base + place[k] + (j % 2 - zbit) * size[k], size[k])]

    def z_copies(k, j, d):
        target = sec + (1 if d == 0 else -1)
        return copy(piece(k, j), piece(k, j), z_send.at[k, d, abs_step(j)], z_recv.at[k, d, abs_step(j, 1)], (me, target))

    def abs_step(j, more=0):
        return more + jnp.where(j > sec, j - sec, sec - j)

    def z_send_item(dist, d):
        j = sec - dist if d == 0 else sec + dist
        target = sec + 1 if d == 0 else sec - 1
        ok = (j >= 0) & (target < n_sec) if d == 0 else (j < n_sec) & (target >= 0)

        @pl.when(ok)
        def _():
            for k in range(len(parts)):
                copy(piece(k, j), piece(k, j), z_send.at[k, d, dist], z_recv.at[k, d, dist], (me, target)).start()

    def z_wait_send(dist, d):
        j = sec - dist if d == 0 else sec + dist
        target = sec + 1 if d == 0 else sec - 1
        ok = (j >= 0) & (target < n_sec) if d == 0 else (j < n_sec) & (target >= 0)

        @pl.when(ok)
        def _():
            for k in range(len(parts)):
                copy(piece(k, j), piece(k, j), z_send.at[k, d, dist], z_recv.at[k, d, dist], (me, target)).wait_send()

    def z_wait_recv(dist, d):
        j = sec - dist - 1 if d == 0 else sec + dist + 1
        target = sec + 1 if d == 0 else sec - 1
        ok = (j >= 0) if d == 0 else (j < n_sec)

        @pl.when(ok)
        def _():
            for k in range(len(parts)):
                copy(piece(k, j), piece(k, j), z_send.at[k, d, dist], z_recv.at[k, d, dist], (me, sec)).wait_recv()

    def region(k, t):
        order = orders[k]
        off, n = jnp.int32(parts[k][0]), parts[k][1]
        for j in order[:len(order) - t]:
            n = n // 2
            off = off + bit[j] * n
        return off, n

    def g_copy(which, k, t, l):
        off, n = region(k, t)
        j = orders[k][len(orders[k]) - 1 - t]
        ref = full.at[l, rows(base + off, n)]
        return copy(ref, ref, g_send.at[which, k, t], g_recv.at[which, k, t], peer(j))

    def c_copy(which, l):
        ref = full.at[l, rows(base, half)]
        return copy(ref, ref, g_send.at[which, 0, nb - 1], g_recv.at[which, 0, nb - 1], peer(0))

    n_layer = n_sec // 2
    layers = [layer] + [(layer + i) % n_layer for i in range(1, n_layer)]
    steps = nb - 1
    for d in range(2):
        z_send_item(0, d)
    for d in range(2):
        z_wait_recv(0, d)
    for d in range(2):
        z_send_item(1, d)
    for k in range(len(parts)):
        g_copy(0, k, 0, layers[0]).start()
    for dist in range(1, n_sec - 1):
        for d in range(2):
            z_wait_recv(dist, d)
        if dist < n_sec - 2:
            for d in range(2):
                z_send_item(dist + 1, d)
        if dist <= steps:
            for k in range(len(parts)):
                g_copy(0, k, dist - 1, layers[0]).wait_recv()
                if dist < steps:
                    g_copy(0, k, dist, layers[0]).start()
    done = min(n_sec - 2, steps)
    for t in range(done, steps):
        for k in range(len(parts)):
            g_copy(0, k, t, layers[0]).wait_recv()
            if t + 1 < steps:
                g_copy(0, k, t + 1, layers[0]).start()
    c_copy(0, layers[0]).start()
    for w in range(1, n_layer):
        for t in range(steps):
            for k in range(len(parts)):
                g_copy(w, k, t, layers[w]).start()
            for k in range(len(parts)):
                g_copy(w, k, t, layers[w]).wait_recv()
        c_copy(w, layers[w]).start()
    for w in range(n_layer):
        c_copy(w, layers[w]).wait_recv()
    for w in range(n_layer):
        for t in range(steps):
            for k in range(len(parts)):
                g_copy(w, k, t, layers[w]).wait_send()
        c_copy(w, layers[w]).wait_send()
    for dist in range(n_sec - 1):
        for d in range(2):
            z_wait_send(dist, d)


def reduce_call(n_dp, n_sec, grads):
    rows, width = grads.shape
    nb = bits_of(n_dp)
    vm = pl.BlockSpec(memory_space=pltpu.VMEM)
    return pl.pallas_call(
        functools.partial(reduce_kernel, n_dp, n_sec),
        in_specs=[vm],
        out_specs=vm,
        out_shape=jax.ShapeDtypeStruct((n_sec // 2, rows, width), bf16),
        scratch_shapes=[
            pltpu.VMEM((rows // 2, width), bf16), pltpu.VMEM((rows, width), bf16),
            pltpu.SemaphoreType.DMA((2, nb + 1)), pltpu.SemaphoreType.DMA((2, nb + 1)),
            pltpu.SemaphoreType.DMA((2, 2, n_sec)), pltpu.SemaphoreType.DMA((2, 2, n_sec)),
            pltpu.SemaphoreType.DMA((n_sec // 2, 2, nb)), pltpu.SemaphoreType.DMA((n_sec // 2, 2, nb)),
        ],
        compiler_params=pltpu.CompilerParams(collective_id=1, has_side_effects=True, vmem_limit_bytes=48 * 2**20),
        name="reduce",
    )(grads)


def finish_kernel(P, full, scale_o, shift_o, gain_o, pw_o, off_o, up_o, upb_o, down_o, dnb_o):
    L = pw_o.shape[1]
    D, H = up_o.shape[1:]
    step = pl.program_id(0)
    for k in range(0, H, D):
        up_o[0, :, k:k + D] = full[0, k:k + D, :].astype(f32)
    down_o[0] = full[0, H:2 * H, :].astype(f32)
    tail = full[0, 2 * H:2 * H + up_to(P + SMALL_ROWS, 16), :].astype(f32)
    small = tail[P:P + SMALL_ROWS, :]
    for l in range(L):
        @pl.when(step == l)
        def _():
            pw_o[:, l, :] = tail[0:P, 0:P]
            for out, row in ((scale_o, ROW_SCALE), (shift_o, ROW_SHIFT), (gain_o, ROW_GAIN)):
                out[2 * l:2 * l + 2, :] = small[row:row + 2, :]
            off_o[l:l + 1, :] = small[ROW_OFFSET:ROW_OFFSET + 1, 0:P]
            for k in range(H // D):
                upb_o[l:l + 1, k * D:(k + 1) * D] = small[ROW_UPB + k:ROW_UPB + k + 1, :]
            dnb_o[l:l + 1, :] = small[ROW_UPB + H // D:ROW_UPB + H // D + 1, :]


def finish_call(full, P, H):
    L, rows, D = full.shape
    const = lambda *shape: pl.BlockSpec(shape, lambda i: (0,) * len(shape))
    return pl.pallas_call(
        functools.partial(finish_kernel, P),
        grid=(L,),
        in_specs=[pl.BlockSpec((1, rows, D), lambda i: (i, 0, 0))],
        out_specs=[const(2 * L, D), const(2 * L, D), const(2 * L, D), const(P, L, P), const(L, P),
                   pl.BlockSpec((1, D, H), lambda i: (i, 0, 0)), const(L, H), pl.BlockSpec((1, H, D), lambda i: (i, 0, 0)), const(L, D)],
        out_shape=[jax.ShapeDtypeStruct(s, f32) for s in ((2 * L, D), (2 * L, D), (2 * L, D), (P, L, P), (L, P), (L, D, H), (L, H), (L, H, D), (L, D))],
        compiler_params=pltpu.CompilerParams(vmem_limit_bytes=40 * 2**20),
        name="finish",
    )(full)


def shards(n_dp, n_sec, images, out_grad, padding, affine_scale, affine_shift, layer_scale, patch_weight, patch_bias, up_weight, up_bias, down_weight, down_bias):
    n_patch, width = images.shape[2:]
    hidden = up_weight.shape[2]
    grad_rows = up_to(2 * hidden + n_patch + SMALL_ROWS, 2 * reduce_unit(n_dp))
    outputs, in_grads, grads = compute_call(
        lambda: lax.axis_index("section"), grad_rows,
        images.transpose(0, 2, 1, 3), out_grad.transpose(0, 2, 1, 3), padding.T,
        affine_scale, affine_shift, layer_scale, patch_weight.transpose(1, 0, 2), patch_bias,
        up_weight, up_bias, down_weight, down_bias,
    )
    full = reduce_call(n_dp, n_sec, grads)
    scale, shift, gain, slopes, offset, up, upb, down, dnb = finish_call(full, n_patch, hidden)
    native = lambda a: a.transpose(0, 2, 1, 3)[None]
    return native(outputs), native(in_grads), scale, shift, gain, slopes.transpose(1, 0, 2), offset, up, upb, down, dnb


def solution(mesh):
    split = P(None, "dp", None, None)
    return jax.shard_map(
        functools.partial(shards, mesh.shape["dp"], mesh.shape["section"]),
        mesh=mesh,
        in_specs=(split, split, P(None, "dp")) + (P(),) * 9,
        out_specs=(P("section", None, "dp", None, None),) * 2 + (P(),) * 9,
        check_vma=False,
    )
```

time: 809 us -> 183 us (0.23)
  waiting for transfers between devices: 351 us -> 0 us
  Pallas kernels: 0 us -> 178 us
  local copies, waits for them, and re-layouts: 160 us -> 4.16 us
  other arithmetic: 119 us -> 0 us
  starting transfers between devices: 80.6 us -> 0 us
  blocking collectives: 43.6 us -> 0 us
  matrix products: 32.5 us -> 0 us
  between operations: 14.3 us -> 0.68 us
    ppermute x18 -> x0, waiting for transfers between devices: 197 us -> none  [from_behind(): lax.ppermute(value, axis, [(source, source + steps) for source in range(i...]
    pallas_call x0 -> x3, Pallas kernels: none -> 178 us  [the longest x1 112 us: compute_call(): pl.pallas_call(functools.partial(compute_kernel, NC, RC, get_sec), in_spe...]
    psum x1 -> x0, waiting for transfers between devices: 154 us -> none  [shards(): lax.psum((on_section * g_alpha, on_section * g_beta, on_section * g_gain,...]
    ppermute x18 -> x0, starting transfers between devices: 80.5 us -> none  [from_behind(): lax.ppermute(value, axis, [(source, source + steps) for source in range(i...]
    dynamic_slice x46 -> x0, local copies, waits for them, and re-layouts: 54.9 us -> none  [the longest x18 20.1 us: backward_tick(): kept[slot]]
    add x63 -> x0, other arithmetic: 52.8 us -> none  [backward_tick(): totals = jax.tree.map(lambda left, right: left + right, totals, grads)]
    psum x1 -> x0, blocking collectives: 43.6 us -> none  [shards(): lax.psum((on_section * g_alpha, on_section * g_beta, on_section * g_gain,...]
    while x225 -> x0, local copies, waits for them, and re-layouts: 40 us -> none
  transfers between devices with their start and end apart: 19 -> 0, of which waited for: 19 -> 0; matrix products, arithmetic and copies ran while one was open for 12% -> 0% of each run, Pallas kernels for 0% -> 0%
where the time goes in v1:
time: 183 us
  Pallas kernels  178 us (97%)
  local copies, waits for them, and re-layouts  4.16 us (2%)
    pallas_call x1, Pallas kernels, compute_call(): pl.pallas_call(functools.partial(compute_kernel, NC, RC, get_sec), in_spe...  112 us
    pallas_call x1, Pallas kernels, reduce_call(): pl.pallas_call(functools.partial(reduce_kernel, n_dp, n_sec), in_specs=[v...  61.9 us
    pallas_call x1, Pallas kernels, finish_call(): pl.pallas_call(functools.partial(finish_kernel, P), grid=(L,), in_specs=[...  4.19 us
    unnamed x4, local copies, waits for them, and re-layouts  4.16 us

profile of v1, /device:TPU:0, one launch (start us, length us, event | category | flops | bytes accessed | tf_op | source)
XLA Modules:
  0.0 183.0 jit_solution(11562238882879356997)
XLA Ops:
  0.6 112.1 %chain.1 = (bf16[6,196,4,384]{3,2,1,0:T(4,128)(2,1)}, bf16[6,196,4,384]{3,2,1,0:T(4,128)(2,1)}, bf16[3328,384]{1,0:T(8,128)(2,1)}) custom-call(s32[4,6]{1,0:T(4,128)} %bitcast.14, bf16[6,196,4,384]{3,2,1,0:T(4,128)(2,1)} %bitcast.11, bf16[6,196,4,384]{3,2,1,0:T(4,128)(2,1)} %bitcast.12, bf16[4,384]{1,0:T(4,128)(2,1)} %ac.1, bf16[4,384]{1,0:T(4,128)(2,1)} %sh.1, ...), custom_call_target="tpu_custom_call" | custom-call | tf_op jit(solution)/shard_map/chain/pallas_call | solution.py:296
  112.8 0.0 copy-start.1
  112.8 1.7 copy-done.1
  114.5 61.9 %reduce.1.full = bf16[2,3328,384]{2,1,0:T(8,128)(2,1)} custom-call(bf16[3328,384]{1,0:T(8,128)(2,1)S(1)} %copy-done.1), custom_call_target="tpu_custom_call" | custom-call | tf_op jit(solution)/shard_map/reduce/pallas_call | solution.py:506
  176.4 0.0 copy-start
  176.4 2.4 %copy-done = bf16[2,3328,384]{2,1,0:T(8,128)(2,1)S(1)} copy-done((bf16[2,3328,384]{2,1,0:T(8,128)(2,1)S(1)}, bf16[2,3328,384]{2,1,0:T(8,128)(2,1)}, u32[]{:S(2)}) %copy-start) | copy-done | bytes 5111832
  178.9 4.2 %finish.1 = (f32[4,384]{1,0:T(4,128)}, f32[4,384]{1,0:T(4,128)}, f32[4,384]{1,0:T(4,128)}, f32[196,2,196]{2,1,0:T(2,128)}, f32[2,196]{1,0:T(2,128)}, /*index=5*/...) custom-call(bf16[2,3328,384]{2,1,0:T(8,128)(2,1)S(1)} %copy-done), custom_call_target="tpu_custom_call" | custom-call | tf_op jit(solution)/shard_map/finish/pallas_call | solution.py:546
Async XLA Ops:
  112.8 1.7 copy-start.1
  176.4 2.5 %copy-start = (bf16[2,3328,384]{2,1,0:T(8,128)(2,1)S(1)}, bf16[2,3328,384]{2,1,0:T(8,128)(2,1)}, u32[]{:S(2)}) copy-start(bf16[2,3328,384]{2,1,0:T(8,128)(2,1)} %reduce.1.full) | copy-start | bytes 15335428

commit v2 on v1

--- a/solution.py
+++ b/solution.py
@@ -32,26 +32,18 @@
     return hx + hx * t, (half + half * t) + hx * (one - t * t) * (c0 + c03 * square)
 
 
-def plan(sec, t, M):
-    half = M // 2
-    mine = t < half
-    m = lax.rem(t + half * lax.rem(sec, 2), M)
-    yes = sec >= 0
-    return dict(
-        m=m, mine=mine, ffn0=yes, patch1=yes, up1=yes, down1=sec == 3,
-        back_ffn1=yes, back_patch1=(sec < 3) | mine, back_ffn0=sec < 2, back_patch0=(sec == 0) | ((sec == 1) & mine),
-    )
-
-
-def compute_kernel(NC, RC, get_sec, live_ref, img_h, og_h, ac, sh, ls, pw_in, pb_in, wu_h, bu, wd_h, bd, out_h, gin_h, grad_o,
-                   img, og, outs, gins, wu, wd, pw, rs, kk, aa, bdl, wus, wds, bus, stage, xw, xt, gw, gt, hid, slope, dpre,
-                   gx, gd, gp, gsum, sd, bup, gdn, in_sem, out_sem, w_sem):
+def compute_kernel(live_ref, img_h, og_h, ac, sh, ls, pw_in, pb_in, wu_h, bu, wd_h, bd, out_h, gin_h, grad_o,
+                   img, og, outs, gins, xch, pw, rs, kk, aa, bdl, wus, wds, bus, stage, xw, xt, gw, gt, hid, slope, dpre,
+                   gx, gd, gp, gsum, sd, bup, gdn, in_sem, out_sem, w_sem, send_sem, recv_sem):
     M, P, B, D = img.shape
-    L, _, H = wu.shape
+    L, _, H = wus.shape
     PP = pw.shape[1]
     R = B * PP
-    sec = get_sec()
-    own = sec // 2
+    me, sec = lax.axis_index("dp"), lax.axis_index("section")
+    own, odd = sec // 2, sec % 2
+    low = sec < 2
+    partner = (me, sec + 1 - 2 * odd)
+    half = M // 2
 
     def rows(b):
         return slice(b * PP, (b + 1) * PP)
@@ -62,13 +54,24 @@
     def vec(ref, k):
         return ref[k:k + 1, :].astype(f32)
 
+    def micro(t):
+        return lax.rem(t + half * odd, M)
+
     def load(t, which):
-        m = plan(sec, t, M)["m"]
+        m = micro(t)
         return pltpu.make_async_copy((img_h, og_h)[which].at[m], (img, og)[which].at[m], in_sem.at[which, m])
 
+    def save(which, m):
+        return pltpu.make_async_copy((outs, gins)[which].at[m], (out_h, gin_h)[which].at[m], out_sem.at[which, m])
+
+    def remote(src, dst, t):
+        return pltpu.make_async_remote_copy(src_ref=src, dst_ref=dst, send_sem=send_sem.at[t], recv_sem=recv_sem.at[t], device_id=partner, device_id_type=pl.DeviceIdType.MESH)
+
+    barrier = pltpu.get_barrier_semaphore()
+    pl.semaphore_signal(barrier, inc=1, device_id=partner, device_id_type=pl.DeviceIdType.MESH)
     load(0, 0).start()
-    w_up = pltpu.make_async_copy(wu_h, wu, w_sem.at[0])
-    w_down = pltpu.make_async_copy(wd_h, wd, w_sem.at[1])
+    w_up = pltpu.make_async_copy(wu_h, wus, w_sem.at[0])
+    w_down = pltpu.make_async_copy(wd_h, wds, w_sem.at[1])
     w_up.start()
     w_down.start()
     load(0, 1).start()
@@ -95,9 +98,10 @@
         acol = jnp.broadcast_to(vec(ac, 2 * l + 1), (8, D)).T[:, 0:1]
         shift8 = jnp.broadcast_to(vec(sh, 2 * l + 1), (8, D)).astype(bf16)
         for k in range(0, H, D):
-            wus[l, :, k:k + D] = (wu[l, :, k:k + D].astype(f32) * acol).astype(bf16)
-            wds[l, k:k + D, :] = (wd[l, k:k + D, :].astype(f32) * vec(ls, 2 * l + 1)).astype(bf16)
-            bus[l, :, k:k + D] = dot(shift8, wu[l, :, k:k + D])[0:1, :] + bu[l:l + 1, k:k + D].astype(f32)
+            bus[l, :, k:k + D] = dot(shift8, wus[l, :, k:k + D])[0:1, :] + bu[l:l + 1, k:k + D].astype(f32)
+            wus[l, :, k:k + D] = (wus[l, :, k:k + D].astype(f32) * acol).astype(bf16)
+            wds[l, k:k + D, :] = (wds[l, k:k + D, :].astype(f32) * vec(ls, 2 * l + 1)).astype(bf16)
+    pl.semaphore_wait(barrier, 1)
 
     def take(ref, m):
         v = jnp.swapaxes(ref[m].astype(f32), 0, 1)
@@ -105,132 +109,141 @@
             stage[b * PP:b * PP + P, :] = v[b] * live_ref[b, m].astype(f32)
             stage[b * PP + P:(b + 1) * PP, :] = jnp.zeros((PP - P, D), f32)
 
-    def give(which, m, pieces):
-        v = jnp.stack([p[0:P, :] for p in pieces], axis=0)
-        (outs, gins)[which][m] = jnp.swapaxes(v, 0, 1).astype(bf16)
-        pltpu.make_async_copy((outs, gins)[which].at[m], (out_h, gin_h)[which].at[m], out_sem.at[which, m]).start()
-
-    def chunk(c):
-        return pl.ds(pl.multiple_of(c * NC, NC), NC)
-
-    def row_chunk(r):
-        return pl.ds(pl.multiple_of(r * RC, RC), RC)
+    def turned(pieces):
+        return jnp.swapaxes(jnp.stack([p[0:P, :] for p in pieces], axis=0), 0, 1).astype(bf16)
+
+    def from_tall(value):
+        value = value.astype(f32)
+        return turned([value[rows(b), :] for b in range(B)])
+
+    def from_wide(value):
+        return turned([value[:, cols(b)].astype(f32) for b in range(B)])
+
+    def patch_forward(l):
+        mix = dot(pw[l], xw[l])
+        new = [xw[l, :, cols(b)].astype(f32) + (aa[l] * mix[:, cols(b)] + kk[l]) for b in range(B)]
+        xt[l] = jnp.concatenate(new, axis=0).astype(bf16)
+
+    def ffn_forward(l):
+        x = xt[l]
+        h, s = gelu_parts(dot(x, wus[l]) + bus[l])
+        hid[l] = h
+        slope[l] = s
+        new = x.astype(f32) + (dot(h, wds[l]) + bdl[l])
+        for b in range(B):
+            xw[l + 1, :, cols(b)] = new[rows(b), :].astype(bf16)
+
+    def ffn_up(l):
+        h, s = gelu_parts(dot(xt[l], wus[l]) + bus[l])
+        hid[l] = h
+        slope[l] = s
+
+    def back(l, weights):
+        g = gt[l + 1]
+        d = (dot(g, wds[l], 1, 1) * slope[l].astype(f32)).astype(bf16)
+        dpre[...] = d
+        new = g.astype(f32) + dot(d, wus[l], 1, 1)
+        for b in range(B):
+            gw[:, cols(b)] = new[rows(b), :].astype(bf16)
+        back = dot(pw[l], gw[...], 0, 0)
+        new = [gw[:, cols(b)].astype(f32) + aa[l] * back[:, cols(b)] for b in range(B)]
+        gt[l] = jnp.concatenate(new, axis=0).astype(bf16)
+
+        @pl.when(weights)
+        def _():
+            gdn[...] += jnp.sum(g.astype(f32), axis=0, keepdims=True)
+            gx[...] += dot(xt[l].T, dpre[...])
+            gd[...] += dot(gt[l + 1].T, hid[l])
+            bup[...] += jnp.sum(dpre[...].astype(f32), axis=0, keepdims=True)
+            scaled = jnp.concatenate([(gw[:, cols(b)].astype(f32) * aa[l]).astype(bf16) for b in range(B)], axis=1)
+            gp[...] += dot(scaled, xw[l], 1, 1)
+            mix = dot(pw[l], xw[l])
+            for b in range(B):
+                gb = gw[:, cols(b)].astype(f32)
+                gsum[...] += gb
+                sd[...] += jnp.sum(gb * mix[:, cols(b)], axis=0, keepdims=True)
 
     def step(t, carry):
-        p = plan(sec, t, M)
-        m = p["m"]
+        m = micro(t)
+        other = lax.rem(m + half, M)
+        mine = t < half
+        slot = lax.rem(t, half)
+        given = (sec == 3) & jnp.logical_not(mine)
         load(t, 0).wait()
-        take(img, m)
-        for b in range(B):
-            xw[0, :, cols(b)] = stage[rows(b), :].astype(bf16)
-
-        def forward(l, carry):
-            @pl.when((l == 0) | p["patch1"])
+
+        @pl.when(jnp.logical_not(given))
+        def _():
+            take(img, m)
+            for b in range(B):
+                xw[0, :, cols(b)] = stage[rows(b), :].astype(bf16)
+            patch_forward(0)
+            ffn_forward(0)
+
+        @pl.when(sec == 0)
+        def _():
+            outs[m] = from_tall(xt[0])
+
+        @pl.when(sec == 1)
+        def _():
+            outs[m] = from_wide(xw[1])
+
+        @pl.when(given)
+        def _():
+            remote(xch.at[slot], xch.at[slot], slot).wait_recv()
+            xt[1] = xch[slot]
+
+        @pl.when((mine | (sec == 2)))
+        def _():
+            patch_forward(1)
+
+        @pl.when((low & mine) | ((sec == 2) & mine))
+        def _():
+            ffn_up(1)
+
+        @pl.when(sec == 2)
+        def _():
+            outs[m] = from_tall(xt[1])
+
+            @pl.when(mine)
             def _():
-                mix = dot(pw[l], xw[l])
-                new = [xw[l, :, cols(b)].astype(f32) + (aa[l] * mix[:, cols(b)] + kk[l]) for b in range(B)]
-                xt[l] = jnp.concatenate(new, axis=0).astype(bf16)
-
-                @pl.when(sec == 2 * l)
+                xch[slot] = xt[1]
+                remote(xch.at[slot], xch.at[slot], slot).start()
+
+        @pl.when(sec == 3)
+        def _():
+            ffn_forward(1)
+            outs[m] = from_wide(xw[2])
+
+        save(0, m).start()
+        load(t, 1).wait()
+
+        @pl.when(mine | (sec == 3))
+        def _():
+            take(og, m)
+            gt[L] = stage[...].astype(bf16)
+            back(1, (sec > 1) & mine)
+
+            @pl.when(sec == 3)
+            def _():
+                gins[m] = from_wide(gw[...])
+
+                @pl.when(mine)
                 def _():
-                    give(0, m, new)
-
-            @pl.when(jnp.where(l == 0, p["ffn0"], p["up1"]))
+                    gins[M + slot] = from_tall(gt[1])
+                    remote(gins.at[M + slot], gin_h.at[m], slot).start()
+
+            @pl.when(sec == 2)
             def _():
-                def up(c, carry):
-                    pre = dot(xt[l], wus[l, :, chunk(c)]) + bus[l, :, chunk(c)]
-                    h, s = gelu_parts(pre)
-                    hid[l, :, chunk(c)] = h
-                    slope[l, :, chunk(c)] = s
-                    return carry
-                lax.fori_loop(0, H // NC, up, 0)
-
-            @pl.when(jnp.where(l == 0, p["ffn0"], p["down1"]))
+                gins[m] = from_tall(gt[1])
+
+            @pl.when(low)
             def _():
-                def down(r, carry):
-                    q = row_chunk(r)
-                    stage[q, :] = xt[l, q, :].astype(f32) + (dot(hid[l, q, :], wds[l]) + bdl[l])
-                    return carry
-                lax.fori_loop(0, R // RC, down, 0)
-
-                @pl.when(l + 1 < L)
-                def _():
-                    for b in range(B):
-                        xw[l + 1, :, cols(b)] = stage[rows(b), :].astype(bf16)
-
-                @pl.when(sec == 2 * l + 1)
-                def _():
-                    give(0, m, [stage[rows(b), :] for b in range(B)])
-            return carry
-
-        lax.fori_loop(0, L, forward, 0)
-
-        load(t, 1).wait()
-
-        @pl.when(p["back_ffn1"])
-        def _():
-            take(og, m)
-            gt[...] = stage[...].astype(bf16)
-
-        def backward(i, carry):
-            l = L - 1 - i
-            weights = p["mine"] & (own == l)
-
-            @pl.when(jnp.where(l == 0, p["back_ffn0"], p["back_ffn1"]))
-            def _():
-                def dh(c, carry):
-                    d = dot(gt[...], wds[l, chunk(c), :], 1, 1)
-                    dpre[:, chunk(c)] = (d * slope[l, :, chunk(c)].astype(f32)).astype(bf16)
-                    return carry
-                lax.fori_loop(0, H // NC, dh, 0)
-
-                def du(r, carry):
-                    q = row_chunk(r)
-                    stage[q, :] = gt[q, :].astype(f32) + dot(dpre[q, :], wus[l], 1, 1)
-                    return carry
-                lax.fori_loop(0, R // RC, du, 0)
-
-                @pl.when(weights)
-                def _():
-                    gdn[...] += jnp.sum(gt[...].astype(f32), axis=0, keepdims=True)
-                    g_t = gt[...].T
-                    x_t = xt[l].T
-
-                    def grads(c, carry):
-                        q = chunk(c)
-                        d = dpre[:, q]
-                        gx[:, q] += dot(x_t, d)
-                        gd[:, q] += dot(g_t, hid[l, :, q])
-                        bup[:, q] += jnp.sum(d.astype(f32), axis=0, keepdims=True)
-                        return carry
-                    lax.fori_loop(0, H // NC, grads, 0)
-                for b in range(B):
-                    gw[:, cols(b)] = stage[rows(b), :].astype(bf16)
-
-                @pl.when(sec == 2 * l + 1)
-                def _():
-                    give(1, m, [stage[rows(b), :] for b in range(B)])
-
-            @pl.when(jnp.where(l == 0, p["back_patch0"], p["back_patch1"]))
-            def _():
-                back = dot(pw[l], gw[...], 0, 0)
-                new = [gw[:, cols(b)].astype(f32) + aa[l] * back[:, cols(b)] for b in range(B)]
-                gt[...] = jnp.concatenate(new, axis=0).astype(bf16)
-
-                @pl.when(sec == 2 * l)
-                def _():
-                    give(1, m, new)
-
-                @pl.when(weights)
-                def _():
-                    scaled = jnp.concatenate([(gw[:, cols(b)].astype(f32) * aa[l]).astype(bf16) for b in range(B)], axis=1)
-                    gp[...] += dot(scaled, xw[l], 1, 1)
-                    for b in range(B):
-                        gsum[...] += gw[:, cols(b)].astype(f32)
-                        sd[...] += jnp.sum(back[:, cols(b)] * xw[l, :, cols(b)].astype(f32), axis=0, keepdims=True)
-            return carry
-
-        lax.fori_loop(0, L, backward, 0)
+                back(0, low)
+                gins[jnp.where(odd == 0, other, m)] = from_wide(gw[...])
+                gins[jnp.where(odd == 0, m, other)] = from_tall(gt[0])
+                remote(gins.at[other], gin_h.at[m], slot).start()
+
+            save(1, m).start()
         return carry
 
     lax.fori_loop(0, M, step, 0)
@@ -244,16 +257,18 @@
             shift1 = jnp.zeros((D, 1), f32)
             for k in range(0, H, D):
                 g = gx[:, k:k + D]
-                w = wu[l, :, k:k + D].astype(f32)
+                w = wus[l, :, k:k + D].astype(f32)
                 b = bup[:, k:k + D]
                 grad_o[k:k + D, :] = (acol * g + ccol * b).astype(bf16)
                 scale1 += jnp.sum(w * g, axis=1, keepdims=True)
                 shift1 += jnp.sum(w * b, axis=1, keepdims=True)
-            gain1 = vec(bd, l) * gdn[...]
+            gain1 = jnp.zeros((1, D), f32)
             for k in range(0, H, D):
                 g = gd[:, k:k + D].T
-                gain1 += jnp.sum(g * wd[l, k:k + D, :].astype(f32), axis=0, keepdims=True)
+                gain1 += jnp.sum(g * wds[l, k:k + D, :].astype(f32), axis=0, keepdims=True)
                 grad_o[H + k:H + k + D, :] = (g * vec(ls, 2 * l + 1)).astype(bf16)
+            gain1 = gain1 / vec(ls, 2 * l + 1) + vec(bd, l) * gdn[...]
+            scale1, shift1 = scale1 / acol, shift1 / acol
             both = jnp.broadcast_to(jnp.concatenate([scale1, shift1], axis=1), (D, 2)).T
             gs = gsum[...]
             lsrow, crow = vec(ls, 2 * l), vec(sh, 2 * l)
@@ -281,12 +296,28 @@
             put(ROW_UPB + H // D, vec(ls, 2 * l + 1) * gdn[...])
             grad_o[2 * H:2 * H + extra, :] = stage[0:extra, :].astype(bf16)
     grad_o[2 * H + P + SMALL_ROWS:, :] = jnp.zeros((grad_o.shape[0] - 2 * H - P - SMALL_ROWS, D), bf16)
-    for m in range(M):
-        for which in range(2):
-            pltpu.make_async_copy((outs, gins)[which].at[m], (out_h, gin_h)[which].at[m], out_sem.at[which, m]).wait()
-
-
-def compute_call(get_sec, grad_rows, images, out_grad, live, ac, sh, ls, pw, pb, wu, bu, wd, bd, NC=1536, RC=800):
+    for t in range(M):
+        m = micro(t)
+        save(0, m).wait()
+
+        @pl.when((t < half) | (sec == 3))
+        def _():
+            save(1, m).wait()
+    for t in range(half):
+        @pl.when(sec == 2)
+        def _():
+            remote(xch.at[t], xch.at[t], t).wait_send()
+
+        @pl.when(sec != 2)
+        def _():
+            remote(gins.at[t], gin_h.at[t], t).wait_send()
+
+        @pl.when(sec != 3)
+        def _():
+            remote(gins.at[t], gin_h.at[t], t).wait_recv()
+
+
+def compute_call(grad_rows, images, out_grad, live, ac, sh, ls, pw, pb, wu, bu, wd, bd):
     M, P, B, D = images.shape
     L, _, H = wu.shape
     PP = up_to(P, 8)
@@ -294,23 +325,24 @@
     vm = pl.BlockSpec(memory_space=pltpu.VMEM)
     hbm = pl.BlockSpec(memory_space=pl.ANY)
     return pl.pallas_call(
-        functools.partial(compute_kernel, NC, RC, get_sec),
+        compute_kernel,
         in_specs=[pl.BlockSpec(memory_space=pltpu.SMEM), hbm, hbm, vm, vm, vm, vm, vm, hbm, vm, hbm, vm],
         out_specs=[hbm, hbm, vm],
         out_shape=[jax.ShapeDtypeStruct(images.shape, bf16)] * 2 + [jax.ShapeDtypeStruct((grad_rows, D), bf16)],
         scratch_shapes=[
-            pltpu.VMEM(images.shape, bf16), pltpu.VMEM(images.shape, bf16), pltpu.VMEM(images.shape, bf16), pltpu.VMEM(images.shape, bf16),
-            pltpu.VMEM((L, D, H), bf16), pltpu.VMEM((L, H, D), bf16),
+            pltpu.VMEM((M, P, B, D), bf16), pltpu.VMEM((M, P, B, D), bf16), pltpu.VMEM((M, P, B, D), bf16), pltpu.VMEM((M + M // 2, P, B, D), bf16),
+            pltpu.VMEM((M // 2, R, D), bf16),
             pltpu.VMEM((L, PP, PP), bf16), pltpu.VMEM((L, PP, 1), f32), pltpu.VMEM((L, PP, D), f32), pltpu.VMEM((L, 1, D), f32), pltpu.VMEM((L, 1, D), f32),
             pltpu.VMEM((L, D, H), bf16), pltpu.VMEM((L, H, D), bf16), pltpu.VMEM((L, 1, H), f32),
             pltpu.VMEM((R, D), f32),
-            pltpu.VMEM((L, PP, B * D), bf16), pltpu.VMEM((L, R, D), bf16), pltpu.VMEM((PP, B * D), bf16), pltpu.VMEM((R, D), bf16),
+            pltpu.VMEM((L + 1, PP, B * D), bf16), pltpu.VMEM((L, R, D), bf16), pltpu.VMEM((PP, B * D), bf16), pltpu.VMEM((L + 1, R, D), bf16),
             pltpu.VMEM((L, R, H), bf16), pltpu.VMEM((L, R, H), bf16), pltpu.VMEM((R, H), bf16),
             pltpu.VMEM((D, H), f32), pltpu.VMEM((D, H), f32), pltpu.VMEM((PP, PP), f32), pltpu.VMEM((PP, D), f32),
             pltpu.VMEM((1, D), f32), pltpu.VMEM((1, H), f32), pltpu.VMEM((1, D), f32),
             pltpu.SemaphoreType.DMA((2, M)), pltpu.SemaphoreType.DMA((2, M)), pltpu.SemaphoreType.DMA((2,)),
+            pltpu.SemaphoreType.DMA((M // 2,)), pltpu.SemaphoreType.DMA((M // 2,)),
         ],
-        compiler_params=pltpu.CompilerParams(vmem_limit_bytes=60 * 2**20),
+        compiler_params=pltpu.CompilerParams(collective_id=2, has_side_effects=True, vmem_limit_bytes=60 * 2**20),
         name="chain",
     )(live, images, out_grad, ac, sh, ls, pw, pb, wu, bu, wd, bd)
 
@@ -560,7 +592,7 @@
     hidden = up_weight.shape[2]
     grad_rows = up_to(2 * hidden + n_patch + SMALL_ROWS, 2 * reduce_unit(n_dp))
     outputs, in_grads, grads = compute_call(
-        lambda: lax.axis_index("section"), grad_rows,
+        grad_rows,
         images.transpose(0, 2, 1, 3), out_grad.transpose(0, 2, 1, 3), padding.T,
         affine_scale, affine_shift, layer_scale, patch_weight.transpose(1, 0, 2), patch_bias,
         up_weight, up_bias, down_weight, down_bias,

time: 183 us -> 154 us (0.84)
  Pallas kernels: 178 us -> 144 us
  local copies, waits for them, and re-layouts: 4.16 us -> 9.3 us
    pallas_call x1, Pallas kernels: 112 us -> 75.2 us  [compute_call(): pl.pallas_call(compute_kernel, in_specs=[pl.BlockSpec(memory_space=pltpu....]
    unnamed x4 -> x10, local copies, waits for them, and re-layouts: 4.16 us -> 9.3 us
    pallas_call x1, Pallas kernels: 61.9 us -> 64.3 us  [reduce_call(): pl.pallas_call(functools.partial(reduce_kernel, n_dp, n_sec), in_specs=[v...]
where the time goes in v2:
time: 154 us
  Pallas kernels  144 us (94%)
  local copies, waits for them, and re-layouts  9.3 us (6%)
    pallas_call x1, Pallas kernels, compute_call(): pl.pallas_call(compute_kernel, in_specs=[pl.BlockSpec(memory_space=pltpu....  75.2 us
    pallas_call x1, Pallas kernels, reduce_call(): pl.pallas_call(functools.partial(reduce_kernel, n_dp, n_sec), in_specs=[v...  64.3 us
    unnamed x10, local copies, waits for them, and re-layouts  9.3 us
    pallas_call x1, Pallas kernels, finish_call(): pl.pallas_call(functools.partial(finish_kernel, P), grid=(L,), in_specs=[...  4.35 us

profile of v2, /device:TPU:0, one launch (start us, length us, event | category | flops | bytes accessed | tf_op | source)
XLA Modules:
  0.0 153.9 jit_solution(4008275959605923117)
XLA Ops:
  0.6 75.2 %chain.1 = (bf16[6,196,4,384]{3,2,1,0:T(4,128)(2,1)}, bf16[6,196,4,384]{3,2,1,0:T(4,128)(2,1)}, bf16[3328,384]{1,0:T(8,128)(2,1)}) custom-call(s32[4,6]{1,0:T(4,128)} %bitcast.16, bf16[6,196,4,384]{3,2,1,0:T(4,128)(2,1)} %bitcast.11, bf16[6,196,4,384]{3,2,1,0:T(4,128)(2,1)} %bitcast.12, bf16[4,384]{1,0:T(4,128)(2,1)} %ac.1, bf16[4,384]{1,0:T(4,128)(2,1)} %sh.1, ...), custom_call_target="tpu_custom_call" | custom-call | tf_op jit(solution)/shard_map/chain/pallas_call | solution.py:327
  75.8 0.0 copy-start.1
  75.8 1.7 %copy-done.1 = bf16[3328,384]{1,0:T(8,128)(2,1)S(1)} copy-done((bf16[3328,384]{1,0:T(8,128)(2,1)S(1)}, bf16[3328,384]{1,0:T(8,128)(2,1)}, u32[]{:S(2)}) %copy-start.1) | copy-done | bytes 2555928
  77.5 64.3 %reduce.1.full = bf16[2,3328,384]{2,1,0:T(8,128)(2,1)} custom-call(bf16[3328,384]{1,0:T(8,128)(2,1)S(1)} %copy-done.1), custom_call_target="tpu_custom_call" | custom-call | tf_op jit(solution)/shard_map/reduce/pallas_call | solution.py:538
  141.9 0.0 copy-start
  141.9 2.4 %copy-done = bf16[2,3328,384]{2,1,0:T(8,128)(2,1)S(1)} copy-done((bf16[2,3328,384]{2,1,0:T(8,128)(2,1)S(1)}, bf16[2,3328,384]{2,1,0:T(8,128)(2,1)}, u32[]{:S(2)}) %copy-start) | copy-done | bytes 5111832
  144.3 0.0 copy-start.3
  144.3 4.4 %finish.1 = (f32[4,384]{1,0:T(4,128)}, f32[4,384]{1,0:T(4,128)}, f32[4,384]{1,0:T(4,128)}, f32[196,2,196]{2,1,0:T(2,128)}, f32[2,196]{1,0:T(2,128)}, /*index=5*/...) custom-call(bf16[2,3328,384]{2,1,0:T(8,128)(2,1)S(1)} %copy-done), custom_call_target="tpu_custom_call" | custom-call | tf_op jit(solution)/shard_map/finish/pallas_call | solution.py:578
  148.7 0.0 copy-done.3
  148.7 0.0 copy-start.2
  148.7 1.9 %copy.25 = bf16[1,6,4,196,384]{4,2,3,1,0:T(4,128)(2,1)} copy(bf16[1,6,4,196,384]{4,2,3,1,0:T(4,128)(2,1)S(1)} %bitcast.14) | data formatting | bytes 7225344
  150.6 1.5 copy-done.2
  152.0 1.8 %copy.26 = bf16[1,6,4,196,384]{4,2,3,1,0:T(4,128)(2,1)} copy(bf16[1,6,4,196,384]{4,2,3,1,0:T(4,128)(2,1)S(1)} %bitcast.13) | data formatting | bytes 7225344
Async XLA Ops:
  75.8 1.7 %copy-start.1 = (bf16[3328,384]{1,0:T(8,128)(2,1)S(1)}, bf16[3328,384]{1,0:T(8,128)(2,1)}, u32[]{:S(2)}) copy-start(bf16[3328,384]{1,0:T(8,128)(2,1)} %get-tuple-element.25.g_ref) | copy-start | bytes 7667716
  141.9 2.5 %copy-start = (bf16[2,3328,384]{2,1,0:T(8,128)(2,1)S(1)}, bf16[2,3328,384]{2,1,0:T(8,128)(2,1)}, u32[]{:S(2)}) copy-start(bf16[2,3328,384]{2,1,0:T(8,128)(2,1)} %reduce.1.full) | copy-start | bytes 15335428
  144.3 4.4 %copy-start.3 = (bf16[6,196,4,384]{3,2,1,0:T(4,128)(2,1)S(1)}, bf16[6,196,4,384]{3,2,1,0:T(4,128)(2,1)}, u32[]{:S(2)}) copy-start(bf16[6,196,4,384]{3,2,1,0:T(4,128)(2,1)} %get-tuple-element.23) | copy-start | bytes 10838020
  148.7 3.3 %copy-start.2 = (bf16[6,196,4,384]{3,2,1,0:T(4,128)(2,1)S(1)}, bf16[6,196,4,384]{3,2,1,0:T(4,128)(2,1)}, u32[]{:S(2)}) copy-start(bf16[6,196,4,384]{3,2,1,0:T(4,128)(2,1)} %get-tuple-element.24) | copy-start | bytes 10838020

commit v3 on v2

v3 whole, which is shorter than its diff:
```python
import functools

import jax
import jax.numpy as jnp
from jax import lax
from jax.experimental import pallas as pl
from jax.experimental.pallas import tpu as pltpu
from jax.sharding import PartitionSpec as P

f32, bf16 = jnp.float32, jnp.bfloat16
C0 = 0.7978845608028654
C1 = 0.044715
SMALL_ROWS = 12
ROW_SCALE, ROW_SHIFT, ROW_GAIN, ROW_OFFSET, ROW_UPB = 0, 2, 4, 6, 7


def dot(a, b, ca=1, cb=0):
    return lax.dot_general(a, b, (((ca,), (cb,)), ((), ())), preferred_element_type=f32)


def up_to(n, k):
    return -(-n // k) * k


def gelu_parts(pre):
    pre = pre.astype(bf16)
    c0, c01, c03 = bf16(C0), bf16(C0 * C1), bf16(3 * C0 * C1)
    half, one = bf16(0.5), bf16(1.0)
    square = pre * pre
    t = jnp.tanh(pre * (c0 + c01 * square))
    hx = half * pre
    return hx + hx * t, (half + half * t) + hx * (one - t * t) * (c0 + c03 * square)


def bits_of(n):
    return n.bit_length() - 1


def reduce_unit(n_dp):
    return 16 * n_dp


def reduce_parts(half, unit, most=4):
    units = half // unit
    count = min(most, units)
    ends = [units * (k + 1) // count for k in range(count)]
    starts = [0] + ends[:-1]
    return [(a * unit, (b - a) * unit) for a, b in zip(starts, ends)]


def chain_kernel(n_dp, n_sec, live_ref, img_h, og_h, ac, sh, ls, pw_in, pb_in, wu_h, bu, wd_h, bd, out_h, gin_h, full,
                 img, og, xch, pw, rs, kk, aa, bdl, wus, wds, bus, stage, xw, xt, gw, gt, hid, slope, dpre,
                 gx, gd, gp, gsum, sd, bup, gdn, grad_o, work, recv,
                 in_sem, out_sem, w_sem, pair_send, pair_recv, send_sem, recv_sem, z_send, z_recv, g_send, g_recv):
    M, P, B, D = out_h.shape
    L, _, H = wus.shape
    PP = pw.shape[1]
    R = B * PP
    RC = R // 2 if R % 32 == 0 else R
    HC = H // 2 if H % 512 == 0 else H
    me, sec = lax.axis_index("dp"), lax.axis_index("section")
    own, odd = sec // 2, sec % 2
    low = sec < 2
    partner = (me, sec + 1 - 2 * odd)
    half_m = M // 2
    nb = bits_of(n_dp)
    half = full.shape[1] // 2
    parts = reduce_parts(half, reduce_unit(n_dp))
    n_part = len(parts)
    every = range(n_part)
    rest = list(range(1, nb))
    orders = [rest if k % 2 == 0 else rest[::-1] for k in every]
    bit = [(me // (1 << j)) % 2 for j in range(nb)]
    zbit = odd
    base = bit[0] * half

    def peer(j):
        return (me + (1 << j) - 2 * (1 << j) * bit[j], sec)

    def signal(device):
        pl.semaphore_signal(barrier, inc=1, device_id=device, device_id_type=pl.DeviceIdType.MESH)

    def copy(src, dst, s, r, device):
        return pltpu.make_async_remote_copy(src_ref=src, dst_ref=dst, send_sem=s, recv_sem=r, device_id=device, device_id_type=pl.DeviceIdType.MESH)

    def rows(b):
        return slice(b * PP, (b + 1) * PP)

    def span(off, n):
        return pl.ds(pl.multiple_of(off, 128 if n % 128 == 0 and n == HC else 16), n)

    def cols(b):
        return slice(b * D, (b + 1) * D)

    def vec(ref, k):
        return ref[k:k + 1, :].astype(f32)

    def micro(t):
        return lax.rem(t + half_m * odd, M)

    def needs(t, which):
        return (t < half_m) | ((sec == 3) if which else (sec < 3))

    def load(t, which):
        m = micro(t)
        return pltpu.make_async_copy((img_h, og_h)[which].at[m], (img, og)[which].at[m], in_sem.at[which, m])

    def save(which, m):
        return pltpu.make_async_copy((img, og)[which].at[m], (out_h, gin_h)[which].at[m], out_sem.at[which, m])

    def pair(src, dst, t):
        return copy(src, dst, pair_send.at[t], pair_recv.at[t], partner)

    barrier = pltpu.get_barrier_semaphore()
    for j in range(nb):
        signal(peer(j))

    @pl.when(sec > 0)
    def _():
        signal((me, sec - 1))

    @pl.when(sec < n_sec - 1)
    def _():
        signal((me, sec + 1))

    load(0, 0).start()
    w_up = pltpu.make_async_copy(wu_h, wus, w_sem.at[0])
    w_down = pltpu.make_async_copy(wd_h, wds, w_sem.at[1])
    w_up.start()
    w_down.start()
    load(0, 1).start()
    for t in range(1, M):
        for which in range(2):
            @pl.when(needs(t, which))
            def _():
                load(t, which).start()

    pw[...] = jnp.zeros_like(pw)
    pbt = jnp.concatenate([pb_in[...].astype(f32), jnp.zeros((8 - L, P), f32)], axis=0).T
    stage[...] = jnp.zeros_like(stage)
    for l in range(L):
        pw[l, :P, :P] = pw_in[:, l, :]
        rs[l] = jnp.sum(pw[l].astype(f32), axis=1, keepdims=True)
        stage[0:P, l:l + 1] = pbt[:, l:l + 1]
        kk[l] = vec(ls, 2 * l) * (vec(sh, 2 * l) * rs[l] + stage[0:PP, l:l + 1])
        aa[l] = vec(ac, 2 * l) * vec(ls, 2 * l)
        bdl[l] = vec(bd, l) * vec(ls, 2 * l + 1)
    stage[0:PP, 0:128] = jnp.zeros((PP, 128), f32)
    for r in (gx, gd, gp, gsum, sd, bup, gdn):
        r[...] = jnp.zeros_like(r)
    w_up.wait()
    w_down.wait()
    for l in range(L):
        acol = jnp.broadcast_to(vec(ac, 2 * l + 1), (8, D)).T[:, 0:1]
        shift8 = jnp.broadcast_to(vec(sh, 2 * l + 1), (8, D)).astype(bf16)
        for k in range(0, H, D):
            bus[l, :, k:k + D] = dot(shift8, wus[l, :, k:k + D])[0:1, :] + bu[l:l + 1, k:k + D].astype(f32)
            wus[l, :, k:k + D] = (wus[l, :, k:k + D].astype(f32) * acol).astype(bf16)
            wds[l, k:k + D, :] = (wds[l, k:k + D, :].astype(f32) * vec(ls, 2 * l + 1)).astype(bf16)
    pl.semaphore_wait(barrier, nb + jnp.where(sec > 0, 1, 0) + jnp.where(sec < n_sec - 1, 1, 0))

    def take(ref, m):
        v = jnp.swapaxes(ref[m].astype(f32), 0, 1)
        for b in range(B):
            stage[b * PP:b * PP + P, :] = v[b] * live_ref[b, m].astype(f32)
            stage[b * PP + P:(b + 1) * PP, :] = jnp.zeros((PP - P, D), f32)

    def turned(pieces):
        return jnp.swapaxes(jnp.stack([p[0:P, :] for p in pieces], axis=0), 0, 1).astype(bf16)

    def from_tall(value):
        value = value.astype(f32)
        return turned([value[rows(b), :] for b in range(B)])

    def from_wide(value):
        return turned([value[:, cols(b)].astype(f32) for b in range(B)])

    def patch_forward(l):
        mix = dot(pw[l], xw[l])
        new = [xw[l, :, cols(b)].astype(f32) + (aa[l] * mix[:, cols(b)] + kk[l]) for b in range(B)]
        xt[l] = jnp.concatenate(new, axis=0).astype(bf16)

    def ffn_forward(l):
        x = xt[l]
        h, s = gelu_parts(dot(x, wus[l]) + bus[l])
        hid[l] = h
        slope[l] = s
        new = x.astype(f32) + (dot(h, wds[l]) + bdl[l])
        for b in range(B):
            xw[l + 1, :, cols(b)] = new[rows(b), :].astype(bf16)

    def ffn_up(l):
        h, s = gelu_parts(dot(xt[l], wus[l]) + bus[l])
        hid[l] = h
        slope[l] = s

    def ffn_back(l):
        def piece_back(i, carry):
            q = span(i * RC, RC)
            g = gt[l + 1, q, :]
            d = (dot(g, wds[l], 1, 1) * slope[l, q, :].astype(f32)).astype(bf16)
            dpre[q, :] = d
            stage[q, :] = g.astype(f32) + dot(d, wus[l], 1, 1)
            return carry

        lax.fori_loop(0, R // RC, piece_back, 0)
        for b in range(B):
            gw[:, cols(b)] = stage[rows(b), :].astype(bf16)

    def back(l):
        ffn_back(l)
        moved = dot(pw[l], gw[...], 0, 0)
        new = [gw[:, cols(b)].astype(f32) + aa[l] * moved[:, cols(b)] for b in range(B)]
        gt[l] = jnp.concatenate(new, axis=0).astype(bf16)

        @pl.when(own == l)
        def _():
            gdn[...] += jnp.sum(gt[l + 1].astype(f32), axis=0, keepdims=True)
            x_t, g_t = xt[l].T, gt[l + 1].T

            def weight_piece(i, carry):
                q = span(i * HC, HC)
                gx[:, q] += dot(x_t, dpre[:, q])
                gd[:, q] += dot(g_t, hid[l, :, q])
                bup[:, q] += jnp.sum(dpre[:, q].astype(f32), axis=0, keepdims=True)
                return carry

            lax.fori_loop(0, H // HC, weight_piece, 0)
            scaled = jnp.concatenate([(gw[:, cols(b)].astype(f32) * aa[l]).astype(bf16) for b in range(B)], axis=1)
            gp[...] += dot(scaled, xw[l], 1, 1)
            mix = dot(pw[l], xw[l])
            for b in range(B):
                gb = gw[:, cols(b)].astype(f32)
                gsum[...] += gb
                sd[...] += jnp.sum(gb * mix[:, cols(b)], axis=0, keepdims=True)

    def read_images(t, m):
        load(t, 0).wait()
        take(img, m)
        for b in range(B):
            xw[0, :, cols(b)] = stage[rows(b), :].astype(bf16)

    def whole(t, carry):
        m = micro(t)
        other = lax.rem(m + half_m, M)
        read_images(t, m)
        patch_forward(0)
        ffn_forward(0)

        @pl.when(sec == 0)
        def _():
            img[m] = from_tall(xt[0])

        @pl.when(sec == 1)
        def _():
            img[m] = from_wide(xw[1])

        patch_forward(1)

        @pl.when(sec == 2)
        def _():
            img[m] = from_tall(xt[1])
            xch[t] = xt[1]
            pair(xch.at[t], xch.at[t], t).start()

        ffn_up(1)

        @pl.when(sec == 3)
        def _():
            new = xt[1].astype(f32) + (dot(hid[1], wds[1]) + bdl[1])
            img[m] = turned([new[rows(b), :] for b in range(B)])

        save(0, m).start()
        load(t, 1).wait()
        take(og, m)
        gt[L] = stage[...].astype(bf16)

        def half_back(i, carry):
            l = L - 1 - i
            back(l)

            @pl.when(sec == 3)
            def _():
                og[m] = from_wide(gw[...])
                og[M + t] = from_tall(gt[l])
                pair(og.at[M + t], gin_h.at[m], t).start()

            @pl.when(sec == 2)
            def _():
                og[m] = from_tall(gt[l])

            @pl.when(low & (l == 0))
            def _():
                og[jnp.where(odd == 0, other, m)] = from_wide(gw[...])
                og[jnp.where(odd == 0, m, other)] = from_tall(gt[l])
                pair(og.at[other], gin_h.at[m], t).start()
            return carry

        lax.fori_loop(0, jnp.where(low, L, 1), half_back, 0)
        save(1, m).start()
        return carry

    lax.fori_loop(0, half_m, whole, 0)

    for l in range(L):
        @pl.when(own == l)
        def _():
            acol = jnp.broadcast_to(vec(ac, 2 * l + 1), (8, D)).T[:, 0:1]
            ccol = jnp.broadcast_to(vec(sh, 2 * l + 1), (8, D)).T[:, 0:1]
            scale1 = jnp.zeros((D, 1), f32)
            shift1 = jnp.zeros((D, 1), f32)
            for k in range(0, H, D):
                g = gx[:, k:k + D]
                w = wus[l, :, k:k + D].astype(f32)
                b = bup[:, k:k + D]
                grad_o[k:k + D, :] = (acol * g + ccol * b).astype(bf16)
                scale1 += jnp.sum(w * g, axis=1, keepdims=True)
                shift1 += jnp.sum(w * b, axis=1, keepdims=True)
            gain1 = jnp.zeros((1, D), f32)
            for k in range(0, H, D):
                g = gd[:, k:k + D].T
                gain1 += jnp.sum(g * wds[l, k:k + D, :].astype(f32), axis=0, keepdims=True)
                grad_o[H + k:H + k + D, :] = (g * vec(ls, 2 * l + 1)).astype(bf16)
            gain1 = gain1 / vec(ls, 2 * l + 1) + vec(bd, l) * gdn[...]
            scale1, shift1 = scale1 / acol, shift1 / acol
            both = jnp.broadcast_to(jnp.concatenate([scale1, shift1], axis=1), (D, 2)).T
            gs = gsum[...]
            lsrow, crow = vec(ls, 2 * l), vec(sh, 2 * l)
            wsum = jnp.sum(gs * rs[l], axis=0, keepdims=True)
            stage[0:PP, 0:PP] = gp[...] + jnp.sum(gs * (lsrow * crow), axis=1, keepdims=True)
            stage[0:PP, 256:257] = jnp.zeros((PP, 1), f32)
            stage[0:P, 256:257] = pbt[:, l:l + 1]
            psum = jnp.sum(gs * stage[0:PP, 256:257], axis=0, keepdims=True)
            offset = jnp.broadcast_to(jnp.sum(gs * lsrow, axis=1, keepdims=True), (PP, 8)).T[0:1, :]
            s_row = sd[...]
            extra = P + SMALL_ROWS

            def put(k, row):
                stage[P + k:P + k + 1, 0:row.shape[1]] = row
            stage[P:extra, :] = jnp.zeros((SMALL_ROWS, D), f32)
            put(ROW_SCALE, lsrow * s_row)
            put(ROW_SCALE + 1, both[0:1, :])
            put(ROW_SHIFT, lsrow * wsum)
            put(ROW_SHIFT + 1, both[1:2, :])
            put(ROW_GAIN, vec(ac, 2 * l) * s_row + crow * wsum + psum)
            put(ROW_GAIN + 1, gain1)
            put(ROW_OFFSET, offset[:, 0:P])
            for k in range(H // D):
                put(ROW_UPB + k, bup[:, k * D:(k + 1) * D])
            put(ROW_UPB + H // D, vec(ls, 2 * l + 1) * gdn[...])
            grad_o[2 * H:2 * H + extra, :] = stage[0:extra, :].astype(bf16)
    grad_o[2 * H + P + SMALL_ROWS:, :] = jnp.zeros((grad_o.shape[0] - 2 * H - P - SMALL_ROWS, D), bf16)

    def at_step(k, t):
        off, n = jnp.int32(parts[k][0]), parts[k][1]
        for j in orders[k][:t - 1]:
            n = n // 2
            off = off + bit[j] * n
        if t > nb:
            n = n // 2
            off = off + zbit * n
        return off, n

    def exchange(k, t):
        if t == 0:
            off, n = parts[k]
            return copy(grad_o.at[span((1 - bit[0]) * half + off, n)], recv.at[pl.ds(2 * off, n)], send_sem.at[k, 0], recv_sem.at[k, 0], peer(0)), 2 * off
        off, n = at_step(k, t)
        b, device = (bit[orders[k][t - 1]], peer(orders[k][t - 1])) if t < nb else (zbit, partner)
        slot = 2 * parts[k][0] + sum(parts[k][1] >> u for u in range(t))
        return copy(work.at[span(off + (1 - b) * (n // 2), n // 2)], recv.at[pl.ds(slot, n // 2)], send_sem.at[k, t], recv_sem.at[k, t], device), slot

    def add_step(t):
        for k in every:
            c, slot = exchange(k, t)
            c.wait_recv()
            off, n = at_step(k, t + 1)
            piece_rows = parts[k][1] >> nb

            def add(i, carry):
                at = i * piece_rows
                mine = grad_o[span(base + off + at, piece_rows), :] if t == 0 else work[span(off + at, piece_rows), :]
                total = (mine.astype(f32) + recv[span(slot + at, piece_rows), :].astype(f32)).astype(bf16)
                if t < nb:
                    work[span(off + at, piece_rows), :] = total
                else:
                    full[own, span(base + off + at, piece_rows), :] = total
                return carry

            lax.fori_loop(0, n // piece_rows, add, 0)
            if t < nb:
                exchange(k, t + 1)[0].start()
            else:
                for d in range(2):
                    z_send_item(0, d, k)

    place, size = zip(*[at_step(k, nb + 1) for k in every])

    def piece(k, j):
        return full.at[j // 2, span(base + place[k] + (j % 2 - zbit) * size[k], size[k])]

    def z_case(dist, d):
        j, target = (sec - dist, sec + 1) if d == 0 else (sec + dist, sec - 1)
        return j, target, ((j >= 0) & (target < n_sec)) if d == 0 else ((j < n_sec) & (target >= 0))

    def z_copy(dist, d, k, j, target):
        return copy(piece(k, j), piece(k, j), z_send.at[k, d, dist], z_recv.at[k, d, dist], (me, target))

    def z_send_item(dist, d, k):
        j, target, ok = z_case(dist, d)

        @pl.when(ok)
        def _():
            z_copy(dist, d, k, j, target).start()

    def z_wait_send(dist, d, k):
        j, target, ok = z_case(dist, d)

        @pl.when(ok)
        def _():
            z_copy(dist, d, k, j, target).wait_send()

    def z_wait_recv(dist, d, k):
        j = sec - dist - 1 if d == 0 else sec + dist + 1

        @pl.when((j >= 0) & (j < n_sec))
        def _():
            z_copy(dist, d, k, j, sec).wait_recv()

    def region(k, t):
        order = orders[k]
        off, n = jnp.int32(parts[k][0]), parts[k][1]
        for j in order[:len(order) - t]:
            n = n // 2
            off = off + bit[j] * n
        return off, n

    def g_copy(w, k, t, l):
        off, n = region(k, t)
        ref = full.at[l, span(base + off, n)]
        return copy(ref, ref, g_send.at[w, k, t], g_recv.at[w, k, t], peer(orders[k][len(orders[k]) - 1 - t]))

    def c_copy(w, k, l):
        ref = full.at[l, span(base + parts[k][0], parts[k][1])]
        return copy(ref, ref, g_send.at[w, k, nb - 1], g_recv.at[w, k, nb - 1], peer(0))

    layers = [own] + [(own + i) % L for i in range(1, L)]
    steps = nb - 1

    def gather(w, t):
        for k in every:
            g_copy(w, k, t, layers[w]).wait_recv()
            if t + 1 < steps:
                g_copy(w, k, t + 1, layers[w]).start()
            else:
                c_copy(w, k, layers[w]).start()

    def line(dist):
        for k in every:
            for d in range(2):
                z_wait_recv(dist, d, k)
            if dist < n_sec - 2:
                for d in range(2):
                    z_send_item(dist + 1, d, k)
            if dist == 0:
                g_copy(0, k, 0, layers[0]).start()
            if dist == n_sec - 2:
                for w in range(1, L):
                    g_copy(w, k, 0, layers[w]).start()

    waves = [functools.partial(add_step, t) for t in range(nb + 1)]
    waves.append(functools.partial(line, 0))
    for dist in range(1, n_sec - 1):
        waves.append(functools.partial(line, dist))
        if dist <= steps:
            waves.append(functools.partial(gather, 0, dist - 1))
    for t in range(min(n_sec - 2, steps), steps):
        waves.append(functools.partial(gather, 0, t))
    for w in range(1, L):
        for t in range(steps):
            waves.append(functools.partial(gather, w, t))

    def rest_forward(t):
        m = micro(t)

        @pl.when(sec < 3)
        def _():
            read_images(t, m)
            patch_forward(0)

        @pl.when(sec == 0)
        def _():
            img[m] = from_tall(xt[0])

        @pl.when(sec == 3)
        def _():
            slot = t - half_m
            pair(xch.at[slot], xch.at[slot], slot).wait_recv()
            xt[1] = xch[slot]

        @pl.when(sec > 0)
        def _():
            l = jnp.where(sec == 3, 1, 0)
            ffn_forward(l)

            @pl.when(sec != 2)
            def _():
                img[m] = from_wide(xw[l + 1])

        @pl.when(sec == 2)
        def _():
            patch_forward(1)
            img[m] = from_tall(xt[1])

        save(0, m).start()

    def rest_backward(t):
        m = micro(t)

        @pl.when(sec == 3)
        def _():
            load(t, 1).wait()
            take(og, m)
            gt[L] = stage[...].astype(bf16)
            ffn_back(L - 1)
            og[m] = from_wide(gw[...])
            save(1, m).start()

    for k in every:
        exchange(k, 0)[0].start()
    beside = 2 * (M - half_m)

    def rest_step(t, carry):
        for i, piece_of_work in enumerate((rest_forward, rest_backward)):
            piece_of_work(t)
            for n in range(i, min(beside, len(waves)), 2):
                @pl.when(t == half_m + n // 2)
                def _():
                    waves[n]()
        return carry

    lax.fori_loop(half_m, M, rest_step, 0)
    for wave in waves[beside:]:
        wave()
    for w in range(L):
        for k in every:
            c_copy(w, k, layers[w]).wait_recv()

    for k in every:
        for t in range(nb + 1):
            exchange(k, t)[0].wait_send()
        for w in range(L):
            for t in range(steps):
                g_copy(w, k, t, layers[w]).wait_send()
            c_copy(w, k, layers[w]).wait_send()
        for dist in range(n_sec - 1):
            for d in range(2):
                z_wait_send(dist, d, k)
    for t in range(M):
        m = micro(t)
        save(0, m).wait()

        @pl.when((t < half_m) | (sec == 3))
        def _():
            save(1, m).wait()
    for t in range(half_m):
        @pl.when(sec == 2)
        def _():
            pair(xch.at[t], xch.at[t], t).wait_send()

        @pl.when(sec != 2)
        def _():
            pair(og.at[t], gin_h.at[t], t).wait_send()

        @pl.when(sec != 3)
        def _():
            pair(og.at[t], gin_h.at[t], t).wait_recv()


def chain_call(n_dp, n_sec, images, out_grad, live, ac, sh, ls, pw, pb, wu, bu, wd, bd):
    M, P, B, D = images.shape
    L, _, H = wu.shape
    PP = up_to(P, 8)
    R = B * PP
    total = up_to(2 * H + P + SMALL_ROWS, 2 * reduce_unit(n_dp))
    nb = bits_of(n_dp)
    n_part = len(reduce_parts(total // 2, reduce_unit(n_dp)))
    vm = pl.BlockSpec(memory_space=pltpu.VMEM)
    hbm = pl.BlockSpec(memory_space=pl.ANY)
    sem = pltpu.SemaphoreType.DMA
    return pl.pallas_call(
        functools.partial(chain_kernel, n_dp, n_sec),
        in_specs=[pl.BlockSpec(memory_space=pltpu.SMEM), hbm, hbm, vm, vm, vm, vm, vm, hbm, vm, hbm, vm],
        out_specs=[hbm, hbm, vm],
        out_shape=[jax.ShapeDtypeStruct(images.shape, bf16)] * 2 + [jax.ShapeDtypeStruct((L, total, D), bf16)],
        scratch_shapes=[
            pltpu.VMEM((M, P, B, D), bf16), pltpu.VMEM((M + M // 2, P, B, D), bf16), pltpu.VMEM((M // 2, R, D), bf16),
            pltpu.VMEM((L, PP, PP), bf16), pltpu.VMEM((L, PP, 1), f32), pltpu.VMEM((L, PP, D), f32), pltpu.VMEM((L, 1, D), f32), pltpu.VMEM((L, 1, D), f32),
            pltpu.VMEM((L, D, H), bf16), pltpu.VMEM((L, H, D), bf16), pltpu.VMEM((L, 1, H), f32),
            pltpu.VMEM((R, D), f32),
            pltpu.VMEM((L + 1, PP, B * D), bf16), pltpu.VMEM((L, R, D), bf16), pltpu.VMEM((PP, B * D), bf16), pltpu.VMEM((L + 1, R, D), bf16),
            pltpu.VMEM((L, R, H), bf16), pltpu.VMEM((L, R, H), bf16), pltpu.VMEM((R, H), bf16),
            pltpu.VMEM((D, H), f32), pltpu.VMEM((D, H), f32), pltpu.VMEM((PP, PP), f32), pltpu.VMEM((PP, D), f32),
            pltpu.VMEM((1, D), f32), pltpu.VMEM((1, H), f32), pltpu.VMEM((1, D), f32),
            pltpu.VMEM((total, D), bf16), pltpu.VMEM((total // 2, D), bf16), pltpu.VMEM((total, D), bf16),
            sem((2, M)), sem((2, M)), sem((2,)), sem((M // 2,)), sem((M // 2,)),
            sem((n_part, nb + 1)), sem((n_part, nb + 1)), sem((n_part, 2, n_sec)), sem((n_part, 2, n_sec)),
            sem((L, n_part, nb)), sem((L, n_part, nb)),
        ],
        compiler_params=pltpu.CompilerParams(collective_id=1, has_side_effects=True, vmem_limit_bytes=62 * 2**20),
        name="chain",
    )(live, images, out_grad, ac, sh, ls, pw, pb, wu, bu, wd, bd)


def finish_kernel(P, full, scale_o, shift_o, gain_o, pw_o, off_o, up_o, upb_o, down_o, dnb_o):
    L = pw_o.shape[1]
    D, H = up_o.shape[1:]
    step = pl.program_id(0)
    for k in range(0, H, D):
        up_o[0, :, k:k + D] = full[0, k:k + D, :].astype(f32)
    down_o[0] = full[0, H:2 * H, :].astype(f32)
    tail = full[0, 2 * H:2 * H + up_to(P + SMALL_ROWS, 16), :].astype(f32)
    small = tail[P:P + SMALL_ROWS, :]
    for l in range(L):
        @pl.when(step == l)
        def _():
            pw_o[:, l, :] = tail[0:P, 0:P]
            for out, row in ((scale_o, ROW_SCALE), (shift_o, ROW_SHIFT), (gain_o, ROW_GAIN)):
                out[2 * l:2 * l + 2, :] = small[row:row + 2, :]
            off_o[l:l + 1, :] = small[ROW_OFFSET:ROW_OFFSET + 1, 0:P]
            for k in range(H // D):
                upb_o[l:l + 1, k * D:(k + 1) * D] = small[ROW_UPB + k:ROW_UPB + k + 1, :]
            dnb_o[l:l + 1, :] = small[ROW_UPB + H // D:ROW_UPB + H // D + 1, :]


def finish_call(full, P, H):
    L, rows, D = full.shape
    const = lambda *shape: pl.BlockSpec(shape, lambda i: (0,) * len(shape))
    return pl.pallas_call(
        functools.partial(finish_kernel, P),
        grid=(L,),
        in_specs=[pl.BlockSpec((1, rows, D), lambda i: (i, 0, 0))],
        out_specs=[const(2 * L, D), const(2 * L, D), const(2 * L, D), const(P, L, P), const(L, P),
                   pl.BlockSpec((1, D, H), lambda i: (i, 0, 0)), const(L, H), pl.BlockSpec((1, H, D), lambda i: (i, 0, 0)), const(L, D)],
        out_shape=[jax.ShapeDtypeStruct(s, f32) for s in ((2 * L, D), (2 * L, D), (2 * L, D), (P, L, P), (L, P), (L, D, H), (L, H), (L, H, D), (L, D))],
        compiler_params=pltpu.CompilerParams(vmem_limit_bytes=40 * 2**20),
        name="finish",
    )(full)


def shards(n_dp, n_sec, images, out_grad, padding, affine_scale, affine_shift, layer_scale, patch_weight, patch_bias, up_weight, up_bias, down_weight, down_bias):
    outputs, in_grads, full = chain_call(
        n_dp, n_sec,
        images.transpose(0, 2, 1, 3), out_grad.transpose(0, 2, 1, 3), padding.T,
        affine_scale, affine_shift, layer_scale, patch_weight.transpose(1, 0, 2), patch_bias,
        up_weight, up_bias, down_weight, down_bias,
    )
    scale, shift, gain, slopes, offset, up, upb, down, dnb = finish_call(full, images.shape[2], up_weight.shape[2])
    native = lambda a: a.transpose(0, 2, 1, 3)[None]
    return native(outputs), native(in_grads), scale, shift, gain, slopes.transpose(1, 0, 2), offset, up, upb, down, dnb


def solution(mesh):
    split = P(None, "dp", None, None)
    return jax.shard_map(
        functools.partial(shards, mesh.shape["dp"], mesh.shape["section"]),
        mesh=mesh,
        in_specs=(split, split, P(None, "dp")) + (P(),) * 9,
        out_specs=(P("section", None, "dp", None, None),) * 2 + (P(),) * 9,
        check_vma=False,
    )
```

time: 154 us -> 133 us (0.86)
  Pallas kernels: 144 us -> 125 us
  local copies, waits for them, and re-layouts: 9.3 us -> 7.58 us
    pallas_call x2 -> x1, Pallas kernels: 140 us -> 120 us  [chain_call(): pl.pallas_call(functools.partial(chain_kernel, n_dp, n_sec), in_specs=[pl...]
    unnamed x10 -> x8, local copies, waits for them, and re-layouts: 9.3 us -> 7.58 us
where the time goes in v3:
time: 133 us
  Pallas kernels  125 us (94%)
  local copies, waits for them, and re-layouts  7.58 us (6%)
    pallas_call x1, Pallas kernels, chain_call(): pl.pallas_call(functools.partial(chain_kernel, n_dp, n_sec), in_specs=[pl...  120 us
    unnamed x8, local copies, waits for them, and re-layouts  7.58 us
    pallas_call x1, Pallas kernels, finish_call(): pl.pallas_call(functools.partial(finish_kernel, P), grid=(L,), in_specs=[...  4.35 us

profile of v3, /device:TPU:0, one launch (start us, length us, event | category | flops | bytes accessed | tf_op | source)
XLA Modules:
  0.0 132.9 jit_solution(2923583144457596078)
XLA Ops:
  0.6 120.3 %chain.1 = (bf16[6,196,4,384]{3,2,1,0:T(4,128)(2,1)}, bf16[6,196,4,384]{3,2,1,0:T(4,128)(2,1)}, bf16[2,3328,384]{2,1,0:T(8,128)(2,1)}) custom-call(s32[4,6]{1,0:T(4,128)} %bitcast.16, bf16[6,196,4,384]{3,2,1,0:T(4,128)(2,1)} %bitcast.11, bf16[6,196,4,384]{3,2,1,0:T(4,128)(2,1)} %bitcast.12, bf16[4,384]{1,0:T(4,128)(2,1)} %ac.1, bf16[4,384]{1,0:T(4,128)(2,1)} %sh.1, ...), custom_call_target="tpu_custom_call" | custom-call | tf_op jit(solution)/shard_map/chain/pallas_call | solution.py:591
  121.0 0.0 copy-start
  121.0 2.4 %copy-done = bf16[2,3328,384]{2,1,0:T(8,128)(2,1)S(1)} copy-done((bf16[2,3328,384]{2,1,0:T(8,128)(2,1)S(1)}, bf16[2,3328,384]{2,1,0:T(8,128)(2,1)}, u32[]{:S(2)}) %copy-start) | copy-done | bytes 5111832
  123.4 0.0 copy-start.2
  123.4 4.4 %finish.1 = (f32[4,384]{1,0:T(4,128)}, f32[4,384]{1,0:T(4,128)}, f32[4,384]{1,0:T(4,128)}, f32[196,2,196]{2,1,0:T(2,128)}, f32[2,196]{1,0:T(2,128)}, /*index=5*/...) custom-call(bf16[2,3328,384]{2,1,0:T(8,128)(2,1)S(1)} %copy-done), custom_call_target="tpu_custom_call" | custom-call | tf_op jit(solution)/shard_map/finish/pallas_call | solution.py:639
  127.8 0.0 copy-done.2
  127.8 0.0 copy-start.1
  127.8 1.9 %copy.25 = bf16[1,6,4,196,384]{4,2,3,1,0:T(4,128)(2,1)} copy(bf16[1,6,4,196,384]{4,2,3,1,0:T(4,128)(2,1)S(1)} %bitcast.14) | data formatting | bytes 7225344
  129.7 1.5 %copy-done.1 = bf16[6,196,4,384]{3,2,1,0:T(4,128)(2,1)S(1)} copy-done((bf16[6,196,4,384]{3,2,1,0:T(4,128)(2,1)S(1)}, bf16[6,196,4,384]{3,2,1,0:T(4,128)(2,1)}, u32[]{:S(2)}) %copy-start.1) | copy-done | bytes 3612696
  131.1 1.8 %copy.26 = bf16[1,6,4,196,384]{4,2,3,1,0:T(4,128)(2,1)} copy(bf16[1,6,4,196,384]{4,2,3,1,0:T(4,128)(2,1)S(1)} %bitcast.13) | data formatting | bytes 7225344
Async XLA Ops:
  121.0 2.5 %copy-start = (bf16[2,3328,384]{2,1,0:T(8,128)(2,1)S(1)}, bf16[2,3328,384]{2,1,0:T(8,128)(2,1)}, u32[]{:S(2)}) copy-start(bf16[2,3328,384]{2,1,0:T(8,128)(2,1)} %get-tuple-element.25.full) | copy-start | bytes 15335428
  123.4 4.4 %copy-start.2 = (bf16[6,196,4,384]{3,2,1,0:T(4,128)(2,1)S(1)}, bf16[6,196,4,384]{3,2,1,0:T(4,128)(2,1)}, u32[]{:S(2)}) copy-start(bf16[6,196,4,384]{3,2,1,0:T(4,128)(2,1)} %get-tuple-element.23) | copy-start | bytes 10838020
  127.8 3.3 %copy-start.1 = (bf16[6,196,4,384]{3,2,1,0:T(4,128)(2,1)S(1)}, bf16[6,196,4,384]{3,2,1,0:T(4,128)(2,1)}, u32[]{:S(2)}) copy-start(bf16[6,196,4,384]{3,2,1,0:T(4,128)(2,1)} %get-tuple-element.24) | copy-start | bytes 10838020

commit v4 on v3

--- a/solution.py
+++ b/solution.py
@@ -612,40 +612,53 @@
     )(live, images, out_grad, ac, sh, ls, pw, pb, wu, bu, wd, bd)
 
 
-def finish_kernel(P, full, scale_o, shift_o, gain_o, pw_o, off_o, up_o, upb_o, down_o, dnb_o):
+def finish_kernel(P, up_rows, down_rows, tail_rows, x_i, g_i, scale_o, shift_o, gain_o, pw_o, off_o, up_o, upb_o, down_o, dnb_o, x_o, g_o):
     L = pw_o.shape[1]
-    D, H = up_o.shape[1:]
+    D, width = up_o.shape[1:]
     step = pl.program_id(0)
-    for k in range(0, H, D):
-        up_o[0, :, k:k + D] = full[0, k:k + D, :].astype(f32)
-    down_o[0] = full[0, H:2 * H, :].astype(f32)
-    tail = full[0, 2 * H:2 * H + up_to(P + SMALL_ROWS, 16), :].astype(f32)
-    small = tail[P:P + SMALL_ROWS, :]
+    x_o[...] = x_i[...]
+    g_o[...] = g_i[...]
+    for k in range(0, width, D):
+        up_o[0, :, k:k + D] = up_rows[0, k:k + D, :].astype(f32)
+    down_o[...] = down_rows[...].astype(f32)
     for l in range(L):
-        @pl.when(step == l)
-        def _():
+        @pl.when((step == l) & (pl.program_id(1) == 0))
+        def _():
+            tail = tail_rows[0, 0:up_to(P + SMALL_ROWS, 16), :].astype(f32)
+            small = tail[P:P + SMALL_ROWS, :]
             pw_o[:, l, :] = tail[0:P, 0:P]
             for out, row in ((scale_o, ROW_SCALE), (shift_o, ROW_SHIFT), (gain_o, ROW_GAIN)):
                 out[2 * l:2 * l + 2, :] = small[row:row + 2, :]
             off_o[l:l + 1, :] = small[ROW_OFFSET:ROW_OFFSET + 1, 0:P]
-            for k in range(H // D):
+            last = upb_o.shape[1] // D
+            for k in range(last):
                 upb_o[l:l + 1, k * D:(k + 1) * D] = small[ROW_UPB + k:ROW_UPB + k + 1, :]
-            dnb_o[l:l + 1, :] = small[ROW_UPB + H // D:ROW_UPB + H // D + 1, :]
-
-
-def finish_call(full, P, H):
-    L, rows, D = full.shape
-    const = lambda *shape: pl.BlockSpec(shape, lambda i: (0,) * len(shape))
-    return pl.pallas_call(
+            dnb_o[l:l + 1, :] = small[ROW_UPB + last:ROW_UPB + last + 1, :]
+
+
+def finish_call(full, outputs, in_grads, H):
+    L, _, D = full.shape
+    M, P, B, _ = outputs.shape
+    steps = 1
+    shape = (M, P, B, D)
+    n = M // (L * steps)
+    const = lambda *dims: pl.BlockSpec(dims, lambda i, c: (0,) * len(dims))
+    acts = lambda: pl.BlockSpec((n,) + shape[1:], lambda i, c: (i * steps + c, 0, 0, 0))
+    up_spec = pl.BlockSpec((1, D, H // steps), lambda i, c: (i, 0, c))
+    down_spec = pl.BlockSpec((1, H // steps, D), lambda i, c: (i, c, 0))
+    tail = up_to(P + SMALL_ROWS, 256)
+    outs = pl.pallas_call(
         functools.partial(finish_kernel, P),
-        grid=(L,),
-        in_specs=[pl.BlockSpec((1, rows, D), lambda i: (i, 0, 0))],
-        out_specs=[const(2 * L, D), const(2 * L, D), const(2 * L, D), const(P, L, P), const(L, P),
-                   pl.BlockSpec((1, D, H), lambda i: (i, 0, 0)), const(L, H), pl.BlockSpec((1, H, D), lambda i: (i, 0, 0)), const(L, D)],
-        out_shape=[jax.ShapeDtypeStruct(s, f32) for s in ((2 * L, D), (2 * L, D), (2 * L, D), (P, L, P), (L, P), (L, D, H), (L, H), (L, H, D), (L, D))],
-        compiler_params=pltpu.CompilerParams(vmem_limit_bytes=40 * 2**20),
+        grid=(L, steps),
+        in_specs=[pl.BlockSpec((1, H // steps, D), lambda i, c: (i, c, 0)), pl.BlockSpec((1, H // steps, D), lambda i, c: (i, steps + c, 0)),
+                  pl.BlockSpec((1, tail, D), lambda i, c: (i, 2 * H // tail, 0)), acts(), acts()],
+        out_specs=[const(2 * L, D), const(2 * L, D), const(2 * L, D), const(P, L, P), const(L, P), up_spec, const(L, H), down_spec, const(L, D), acts(), acts()],
+        out_shape=[jax.ShapeDtypeStruct(s, f32) for s in ((2 * L, D), (2 * L, D), (2 * L, D), (P, L, P), (L, P), (L, D, H), (L, H), (L, H, D), (L, D))]
+        + [jax.ShapeDtypeStruct(shape, bf16)] * 2,
+        compiler_params=pltpu.CompilerParams(vmem_limit_bytes=62 * 2**20),
         name="finish",
-    )(full)
+    )(full, full, full, outputs.reshape(shape), in_grads.reshape(shape))
+    return tuple(outs[:9]) + tuple(a.reshape(M, P, B, D) for a in outs[9:])
 
 
 def shards(n_dp, n_sec, images, out_grad, padding, affine_scale, affine_shift, layer_scale, patch_weight, patch_bias, up_weight, up_bias, down_weight, down_bias):
@@ -655,7 +668,7 @@
         affine_scale, affine_shift, layer_scale, patch_weight.transpose(1, 0, 2), patch_bias,
         up_weight, up_bias, down_weight, down_bias,
     )
-    scale, shift, gain, slopes, offset, up, upb, down, dnb = finish_call(full, images.shape[2], up_weight.shape[2])
+    scale, shift, gain, slopes, offset, up, upb, down, dnb, outputs, in_grads = finish_call(full, outputs, in_grads, up_weight.shape[2])
     native = lambda a: a.transpose(0, 2, 1, 3)[None]
     return native(outputs), native(in_grads), scale, shift, gain, slopes.transpose(1, 0, 2), offset, up, upb, down, dnb
 

time: 133 us -> 131 us (0.985)
  local copies, waits for them, and re-layouts: 7.58 us -> 0 us
  Pallas kernels: 125 us -> 130 us
    unnamed x8 -> x0, local copies, waits for them, and re-layouts: 7.58 us -> none
    pallas_call x1, Pallas kernels: 4.35 us -> 9.6 us  [finish_call(): pl.pallas_call(functools.partial(finish_kernel, P), grid=(L, steps), in_s...]
where the time goes in v4:
time: 131 us
  Pallas kernels  130 us (99%)
    pallas_call x1, Pallas kernels, chain_call(): pl.pallas_call(functools.partial(chain_kernel, n_dp, n_sec), in_specs=[pl...  120 us
    pallas_call x1, Pallas kernels, finish_call(): pl.pallas_call(functools.partial(finish_kernel, P), grid=(L, steps), in_s...  9.6 us

profile of v4, /device:TPU:0, one launch (start us, length us, event | category | flops | bytes accessed | tf_op | source)
XLA Modules:
  0.0 130.7 jit_solution(16565201104707255707)
XLA Ops:
  0.6 120.3 %chain.1 = (bf16[6,196,4,384]{3,2,1,0:T(4,128)(2,1)}, bf16[6,196,4,384]{3,2,1,0:T(4,128)(2,1)}, bf16[2,3328,384]{2,1,0:T(8,128)(2,1)}) custom-call(s32[4,6]{1,0:T(4,128)} %bitcast.14, bf16[6,196,4,384]{3,2,1,0:T(4,128)(2,1)} %bitcast.11, bf16[6,196,4,384]{3,2,1,0:T(4,128)(2,1)} %bitcast.12, bf16[4,384]{1,0:T(4,128)(2,1)} %ac.1, bf16[4,384]{1,0:T(4,128)(2,1)} %sh.1, ...), custom_call_target="tpu_custom_call" | custom-call | tf_op jit(solution)/shard_map/chain/pallas_call | solution.py:591
  121.0 9.6 %finish.1 = (f32[4,384]{1,0:T(4,128)}, f32[4,384]{1,0:T(4,128)}, f32[4,384]{1,0:T(4,128)}, f32[196,2,196]{2,1,0:T(2,128)}, f32[2,196]{1,0:T(2,128)}, /*index=5*/...) custom-call(bf16[2,3328,384]{2,1,0:T(8,128)(2,1)} %get-tuple-element, ...), custom_call_target="tpu_custom_call" | custom-call | tf_op jit(solution)/shard_map/finish/pallas_call | solution.py:650
